TPU v7x, 32 devices: a whole 2x2x4 slice. The times are simulated.
32 devices in a mesh: dp: 8 (over y, x, core), head: 4 (over z).
Axes of the slice: x: 2, y: 2, z: 4, core: 2. Of those that a mesh axis runs over, the one named last changes fastest.
Arguments:
- text: bfloat16 [16, 2, 492, 768], P('dp', None, 'head'), may hold values from -6 to 6
- boundary: int32 [16, 2, 492], P('dp'), may hold values from 0 to 1, as said below
- reset: int32 [16, 2], P('dp'), may hold values 0 or 1
- memory_in: bfloat16 [16, 10, 768], P('dp'), may hold values from -6 to 6
- init_memory: bfloat16 [10, 768], P(None, ('dp', 'head')), may hold values from -6 to 6
- w_qkv: bfloat16 [768, 3, 768], P(None, None, 'head'), may hold values from -0.21875 to 0.21875
- b_qv: bfloat16 [2, 12, 64], P(None, 'head'), may hold values from -3 to 3
- w_out: bfloat16 [768, 768], P('head'), may hold values from -0.875 to 0.875
- w_in: bfloat16 [768, 3072], P(None, ('dp', 'head')), may hold values from -0.21875 to 0.21875
- w_back: bfloat16 [3072, 768], P(('dp', 'head')), may hold values from -0.109375 to 0.109375
- b_in: bfloat16 [3072], P(('dp', 'head')), may hold values from -3 to 3
- norm_gains: bfloat16 [2, 768], P(None, ('dp', 'head')), may hold values from 0.5 to 1.5
- biases: bfloat16 [4, 768], P(None, ('dp', 'head')), may hold values from -2 to 2
- cotangent: bfloat16 [16, 2, 512, 768], P('dp', None, 'head'), may hold values from -6 to 6
Outputs:
- activations: bfloat16 [16, 2, 512, 768], P('dp', None, 'head')
- d_text: bfloat16 [16, 2, 492, 768], P('dp', None, 'head')
- d_init: float32 [10, 768], P(None, ('dp', 'head'))
- d_w_qkv: float32 [768, 3, 768], P('dp', None, 'head')
- d_b_qv: float32 [2, 12, 64], P(None, 'head', 'dp')
- d_w_out: float32 [768, 768], P('head', 'dp')
- d_w_in: float32 [768, 3072], P(None, ('dp', 'head'))
- d_w_back: float32 [3072, 768], P(('dp', 'head'))
- d_b_in: float32 [3072], P(('dp', 'head'))
- d_norm_gains: float32 [2, 768], P(None, ('dp', 'head'))
- d_biases: float32 [4, 768], P(None, ('dp', 'head'))
Inputs may be any that keep to these rules, and one draw needn't show every extreme that they name: `boundary`: in each aligned block of 2 sequences, one is a single document (it has no document start in either segment), as the data loader pairs one long document with one packed sequence.
All inputs are finite; a program needn't handle non-finite values. No bound on the sum of `reset` on one device may be relied on, other than what follows from the above.
Results may differ from a plain program's by a relative error of at most 0.024.
Values may be sent and summed in bfloat16 or wider, within the bound.
A program may use at most 192 MiB of HBM per device.

v0:
```python
import functools

import jax
import jax.numpy as jnp
from jax import lax
from jax.experimental import pallas as pl
from jax.experimental.pallas import tpu as pltpu
from jax.sharding import PartitionSpec as P

HD = 64
MESH = pl.DeviceIdType.MESH
BF = jnp.bfloat16
F32 = jnp.float32
VMEM_LIMIT = 64 * 1024 * 1024


def nn(a, b):
    return lax.dot_general(a, b, (((1,), (0,)), ((), ())), preferred_element_type=F32)


def nt(a, b):
    return lax.dot_general(a, b, (((1,), (1,)), ((), ())), preferred_element_type=F32)


def tn(a, b):
    return lax.dot_general(a, b, (((0,), (0,)), ((), ())), preferred_element_type=F32)


def place():
    dp, z = lax.axis_index("dp"), lax.axis_index("head")
    core, plane = dp % 2, dp // 2
    return core, plane % 2, plane // 2, z


def device(core, x, y, z):
    return ((y * 2 + x) * 2 + core, z)


def push(src, dst, send, recv, target):
    return pltpu.make_async_remote_copy(
        src_ref=src, dst_ref=dst, send_sem=send, recv_sem=recv, device_id=target, device_id_type=MESH
    )


def from_root(x, axis, root):
    mine = lax.axis_index(axis) == root
    return lax.psum(jnp.where(mine, x, jnp.zeros_like(x)), axis)


def layer_norm(values, gain_row, shift_row):
    center = values - jnp.mean(values, axis=-1, keepdims=True)
    spread = jnp.mean(center * center, axis=-1, keepdims=True)
    return center * lax.rsqrt(spread + 1e-05) * gain_row + shift_row


def gelu_tanh(values):
    return jax.nn.gelu(values, approximate=True)


def head_major(array, dim, dp_count, head_count):
    shape = array.shape
    size = shape[dim]
    split = array.reshape(
        shape[:dim] + (dp_count, head_count, size // (dp_count * head_count)) + shape[dim + 1 :]
    )
    return jnp.swapaxes(split, dim, dim + 1).reshape(shape)


def local(
    text,
    boundary,
    reset,
    memory_in,
    init_memory,
    w_qkv,
    b_qv,
    w_out,
    w_in,
    w_back,
    b_in,
    norm_gains,
    biases,
    cotangent,
):
    head_count = lax.axis_size("head")
    dp_count = lax.axis_size("dp")
    head_idx = lax.axis_index("head")
    batch_size = text.shape[0]
    width = text.shape[3]
    seg_rows = cotangent.shape[2]
    seg_len = seg_rows * head_count
    mem_rows = memory_in.shape[1]
    text_len = seg_len - 2 * mem_rows
    local_width = w_qkv.shape[2]
    local_heads = local_width // HD
    row_start = head_idx * seg_rows
    is_first = (head_idx == 0).astype(jnp.float32)
    is_final = (head_idx == head_count - 1).astype(jnp.float32)
    grad_dims = (1, 0, 0, 1, 1, 1)
    doc_ids = jnp.cumsum(boundary, axis=2)
    marks = jnp.full((batch_size, 2, mem_rows), -1, jnp.int32)
    labels = jnp.concatenate([marks, doc_ids, marks], axis=2)
    visible = (
        (labels[..., :, None] == labels[..., None, :])
        | (labels[..., :, None] < 0)
        | (labels[..., None, :] < 0)
    )
    bias_query = b_qv[0].reshape(local_width).astype(jnp.float32)
    bias_value = b_qv[1].reshape(local_width).astype(jnp.float32)
    shared = (
        lax.all_gather(w_in, ("dp", "head"), axis=1, tiled=True),
        lax.all_gather(w_back, ("dp", "head"), axis=0, tiled=True),
        lax.all_gather(b_in, ("dp", "head"), axis=0, tiled=True),
        lax.all_gather(norm_gains, ("dp", "head"), axis=1, tiled=True),
        lax.all_gather(biases, ("dp", "head"), axis=1, tiled=True),
        lax.all_gather(init_memory, ("dp", "head"), axis=1, tiled=True),
    )

    def fetch():
        return shared

    def attention_probs(query, key_rows, seg):
        scores = (
            jnp.einsum("sqhe,skhe->shqk", query, key_rows, preferred_element_type=jnp.float32)
            * 0.125
        )
        return jnp.where(visible[:, seg][:, None], scores, -1e30)

    def forward(seg, memory, ffn):
        w_in_all, w_back_all, b_in_all, gains_all, biases_all, unused = ffn
        gains_f = gains_all.astype(jnp.float32)
        biases_f = biases_all.astype(jnp.float32)
        local_text = lax.all_gather(text[:, seg], "head", axis=1, tiled=True)
        x_rows = jnp.concatenate([memory, local_text, memory], axis=1)
        mixed = jnp.einsum("srd,dce->srce", x_rows, w_qkv, preferred_element_type=jnp.float32)
        query = (
            (mixed[:, :, 0] + bias_query)
            .astype(jnp.bfloat16)
            .reshape(batch_size, seg_len, local_heads, HD)
        )
        key_rows = mixed[:, :, 1].astype(jnp.bfloat16).reshape(batch_size, seg_len, local_heads, HD)
        value = (
            (mixed[:, :, 2] + bias_value)
            .astype(jnp.bfloat16)
            .reshape(batch_size, seg_len, local_heads, HD)
        )
        masked = attention_probs(query, key_rows, seg)
        row_max = jnp.max(masked, axis=-1, keepdims=True)
        exp_terms = jnp.exp(masked - row_max)
        row_total = jnp.sum(exp_terms, axis=-1, keepdims=True)
        log_total = row_max + jnp.log(row_total)
        probs = (exp_terms / row_total).astype(jnp.bfloat16)
        attended = jnp.einsum("shqk,skhe->sqhe", probs, value, preferred_element_type=jnp.float32)
        attended = attended.astype(jnp.bfloat16).reshape(batch_size, seg_len, local_width)
        partial_out = jnp.einsum("srl,ld->srd", attended, w_out, preferred_element_type=jnp.float32)
        summed = lax.psum_scatter(
            partial_out.astype(jnp.bfloat16), "head", scatter_dimension=1, tiled=True
        ).astype(jnp.float32)
        own_rows = lax.dynamic_slice_in_dim(x_rows, row_start, seg_rows, 1).astype(jnp.float32)
        pre_norm = own_rows + summed + biases_f[1]
        hidden = layer_norm(pre_norm, gains_f[0], biases_f[0])
        hidden_low = hidden.astype(jnp.bfloat16)
        inner = jnp.einsum(
            "srd,df->srf", hidden_low, w_in_all, preferred_element_type=jnp.float32
        ) + b_in_all.astype(jnp.float32)
        active = gelu_tanh(inner).astype(jnp.bfloat16)
        outer = (
            jnp.einsum("srf,fd->srd", active, w_back_all, preferred_element_type=jnp.float32)
            + biases_f[2]
        )
        post_norm = hidden + outer
        result = layer_norm(post_norm, gains_f[1], biases_f[3])
        kept = (
            x_rows,
            query,
            key_rows,
            value,
            log_total,
            attended,
            pre_norm,
            hidden_low,
            inner,
            active,
            post_norm,
        )
        return (result, kept)

    def backward(seg, grad_out, kept, ffn):
        (
            x_rows,
            query,
            key_rows,
            value,
            log_total,
            attended,
            pre_norm,
            hidden_low,
            inner,
            active,
            post_norm,
        ) = kept
        w_in_all, w_back_all, b_in_all, gains_all, biases_all, unused = ffn
        gains_f = gains_all.astype(jnp.float32)
        biases_f = biases_all.astype(jnp.float32)
        unused_two, pull_two = jax.vjp(layer_norm, post_norm, gains_f[1], biases_f[3])
        grad_post, grad_gain_two, grad_shift_two = pull_two(grad_out)
        grad_outer = grad_post.astype(jnp.bfloat16)
        grad_ffn_bias = jnp.sum(grad_post, axis=(0, 1))
        grad_w_back = jnp.einsum(
            "srf,srd->fd", active, grad_outer, preferred_element_type=jnp.float32
        )
        grad_active = jnp.einsum(
            "srd,fd->srf", grad_outer, w_back_all, preferred_element_type=jnp.float32
        )
        unused_gelu, pull_gelu = jax.vjp(gelu_tanh, inner)
        grad_inner = pull_gelu(grad_active)[0].astype(jnp.bfloat16)
        grad_b_in = jnp.sum(grad_inner, axis=(0, 1), dtype=jnp.float32)
        grad_w_in = jnp.einsum(
            "srd,srf->df", hidden_low, grad_inner, preferred_element_type=jnp.float32
        )
        grad_hidden = grad_post + jnp.einsum(
            "srf,df->srd", grad_inner, w_in_all, preferred_element_type=jnp.float32
        )
        unused_one, pull_one = jax.vjp(layer_norm, pre_norm, gains_f[0], biases_f[0])
        grad_pre, grad_gain_one, grad_shift_one = pull_one(grad_hidden)
        grad_out_bias = jnp.sum(grad_pre, axis=(0, 1))
        grad_branch = lax.all_gather(grad_pre.astype(jnp.bfloat16), "head", axis=1, tiled=True)
        grad_w_out = jnp.einsum(
            "srl,srd->ld", attended, grad_branch, preferred_element_type=jnp.float32
        )
        grad_att = jnp.einsum("srd,ld->srl", grad_branch, w_out, preferred_element_type=jnp.float32)
        grad_att = grad_att.astype(jnp.bfloat16).reshape(batch_size, seg_len, local_heads, HD)
        masked = attention_probs(query, key_rows, seg)
        probs = jnp.exp(masked - log_total)
        grad_value = jnp.einsum(
            "shqk,sqhe->skhe",
            probs.astype(jnp.bfloat16),
            grad_att,
            preferred_element_type=jnp.float32,
        )
        grad_probs = jnp.einsum(
            "sqhe,skhe->shqk", grad_att, value, preferred_element_type=jnp.float32
        )
        grad_scores = probs * (grad_probs - jnp.sum(grad_probs * probs, axis=-1, keepdims=True))
        grad_scores = grad_scores.astype(jnp.bfloat16)
        grad_query = (
            jnp.einsum("shqk,skhe->sqhe", grad_scores, key_rows, preferred_element_type=jnp.float32)
            * 0.125
        )
        grad_key = (
            jnp.einsum("shqk,sqhe->skhe", grad_scores, query, preferred_element_type=jnp.float32)
            * 0.125
        )
        grad_mixed = jnp.stack([grad_query, grad_key, grad_value], axis=2).astype(jnp.bfloat16)
        grad_mixed = grad_mixed.reshape(batch_size, seg_len, 3, local_width)
        grad_bias_qv = jnp.stack(
            [
                jnp.sum(grad_mixed[:, :, 0], axis=(0, 1), dtype=jnp.float32),
                jnp.sum(grad_mixed[:, :, 2], axis=(0, 1), dtype=jnp.float32),
            ]
        ).reshape(2, local_heads, HD)
        grad_w_qkv = jnp.einsum(
            "srd,srce->dce", x_rows, grad_mixed, preferred_element_type=jnp.float32
        )
        grad_rows = jnp.einsum(
            "srce,dce->srd", grad_mixed, w_qkv, preferred_element_type=jnp.float32
        )
        placed = lax.dynamic_update_slice_in_dim(jnp.zeros_like(grad_rows), grad_pre, row_start, 1)
        grad_rows = grad_rows + placed
        grad_text_part = lax.psum_scatter(
            grad_rows[:, mem_rows : mem_rows + text_len].astype(jnp.bfloat16),
            "head",
            scatter_dimension=1,
            tiled=True,
        ).astype(jnp.float32)
        grad_memory = lax.psum(
            (grad_rows[:, :mem_rows] + grad_rows[:, seg_len - mem_rows :]).astype(jnp.bfloat16),
            "head",
        ).astype(jnp.float32)
        reset_flag = reset[:, seg] > 0
        grad_init = (
            jnp.sum(jnp.where(reset_flag[:, None, None], grad_memory, 0.0), axis=0) * is_first
        )
        ffn_grads = (
            grad_w_in,
            grad_w_back,
            grad_b_in,
            jnp.stack([grad_gain_one, grad_gain_two]),
            jnp.stack([grad_shift_one, grad_out_bias, grad_ffn_bias, grad_shift_two]),
            grad_init,
        )
        return (grad_text_part, grad_memory, (grad_w_qkv, grad_bias_qv, grad_w_out), ffn_grads)

    ffn_first = fetch()
    init_all = ffn_first[5]
    memory_one = jnp.where(reset[:, 0, None, None] > 0, init_all[None], memory_in)
    out_one, kept_one = forward(0, memory_one, ffn_first)
    tail_rows = out_one[:, seg_rows - mem_rows :].astype(jnp.bfloat16)
    carried = from_root(tail_rows, "head", head_count - 1)
    ffn_second = fetch()
    memory_two = jnp.where(reset[:, 1, None, None] > 0, ffn_second[5][None], carried)
    out_two, kept_two = forward(1, memory_two, ffn_second)
    activations = jnp.stack([out_one, out_two], axis=1).astype(jnp.bfloat16)
    ffn_third = fetch()
    text_two, memory_grad_two, attn_two, ffn_two = backward(
        1, cotangent[:, 1].astype(jnp.float32), kept_two, ffn_third
    )
    keep_flag = reset[:, 1, None, None] <= 0
    carried_grad = jnp.where(keep_flag, memory_grad_two, 0.0) * is_final
    grad_one = cotangent[:, 0].astype(jnp.float32) + jnp.concatenate(
        [jnp.zeros((batch_size, seg_rows - mem_rows, width), jnp.float32), carried_grad], axis=1
    )
    ffn_fourth = fetch()
    text_one, memory_grad_one, attn_one, ffn_one = backward(0, grad_one, kept_one, ffn_fourth)
    grads = jax.tree.map(lambda a, b: a + b, ffn_one, ffn_two)
    ffn_total = tuple((head_major(g, d, dp_count, head_count) for g, d in zip(grads, grad_dims)))
    partial_sums = (
        lax.psum_scatter(
            ffn_total[0].astype(jnp.bfloat16), "head", scatter_dimension=1, tiled=True
        ).astype(jnp.float32),
        lax.psum_scatter(
            ffn_total[1].astype(jnp.bfloat16), "head", scatter_dimension=0, tiled=True
        ).astype(jnp.float32),
        lax.psum_scatter(
            ffn_total[2].astype(jnp.bfloat16), "head", scatter_dimension=0, tiled=True
        ).astype(jnp.float32),
        lax.psum_scatter(
            ffn_total[3].astype(jnp.bfloat16), "head", scatter_dimension=1, tiled=True
        ).astype(jnp.float32),
        lax.psum_scatter(
            ffn_total[4].astype(jnp.bfloat16), "head", scatter_dimension=1, tiled=True
        ).astype(jnp.float32),
        lax.psum_scatter(
            ffn_total[5].astype(jnp.bfloat16), "head", scatter_dimension=1, tiled=True
        ).astype(jnp.float32),
    )
    reduced = (
        lax.psum_scatter(partial_sums[0], "dp", scatter_dimension=1, tiled=True),
        lax.psum_scatter(partial_sums[1], "dp", scatter_dimension=0, tiled=True),
        lax.psum_scatter(partial_sums[2], "dp", scatter_dimension=0, tiled=True),
        lax.psum_scatter(partial_sums[3], "dp", scatter_dimension=1, tiled=True),
        lax.psum_scatter(partial_sums[4], "dp", scatter_dimension=1, tiled=True),
        lax.psum_scatter(partial_sums[5], "dp", scatter_dimension=1, tiled=True),
    )
    attn_total = jax.tree.map(lambda a, b: a + b, attn_one, attn_two)
    grad_qkv, grad_bqv, grad_wout = (
        lax.psum_scatter(attn_total[0], "dp", scatter_dimension=0, tiled=True),
        lax.psum_scatter(attn_total[1], "dp", scatter_dimension=2, tiled=True),
        lax.psum_scatter(attn_total[2], "dp", scatter_dimension=1, tiled=True),
    )
    grad_text = jnp.stack([text_one, text_two], axis=1).astype(jnp.bfloat16)
    grad_win, grad_wback, grad_bin, grad_gains, grad_biases, grad_init = reduced
    return (
        activations,
        grad_text,
        grad_init,
        grad_qkv,
        grad_bqv,
        grad_wout,
        grad_win,
        grad_wback,
        grad_bin,
        grad_gains,
        grad_biases,
    )


class Refs:
    pass


def by_name(names, values):
    refs = Refs()
    for name, value in zip(names, values, strict=True):
        setattr(refs, name, value)
    return refs


def loop(count, body, unroll=1):
    def run(i, unused):
        body(i)
        return unused

    lax.fori_loop(0, count, run, 0, unroll=unroll)


def add_all(dst, *sources):
    def body(at):
        dst[at] = sum([src[at].astype(F32) for src in sources], dst[at].astype(F32)).astype(BF)

    if len(dst.shape) == 2:
        body(...)
    else:
        loop(dst.shape[0], body)


def as_column(row):
    n = row.shape[1]
    down = lax.broadcasted_iota(jnp.int32, (n, n), 0)
    across = lax.broadcasted_iota(jnp.int32, (n, n), 1)
    return jnp.sum(jnp.where(down == across, row, 0.0), axis=1, keepdims=True)


def norm(v):
    center = v - jnp.mean(v, axis=-1, keepdims=True)
    scale = lax.rsqrt(jnp.mean(center * center, axis=-1, keepdims=True) + 1e-05)
    return center * scale, scale


def pull_norm(g, hat, scale):
    m1 = jnp.mean(g, axis=-1, keepdims=True)
    m2 = jnp.mean(g * hat, axis=-1, keepdims=True)
    return scale * (g - m1 - hat * m2)


def row_sum(v):
    return jnp.sum(v, axis=0, keepdims=True)


def main_kernel(names, dp_count, head_count, *values):
    r_ = by_name(names, values)
    core, px, py, z = place()
    plane = py * 2 + px
    x_plane, y_plane = py * 2 + 1 - px, (1 - py) * 2 + px
    me = (plane * 2 + core) * head_count + z
    total = dp_count * head_count
    planes = dp_count // 2
    is_home = core == z // 2
    away = jnp.logical_not(is_home)
    sibling = device(1 - core, px, py, z)
    x_mate, y_mate = device(core, 1 - px, py, z), device(core, px, 1 - py, z)
    mirror = z // 2

    def from_end(i):
        return i + mirror * (head_count - 1 - 2 * i)

    depth = from_end(z)
    inside = depth == 1
    order = [from_end(i) for i in (depth, 1 - depth, 2, 3)]

    def order_at(n):
        return from_end(jnp.where(n == 0, depth, jnp.where(n == 1, 1 - depth, n)))

    x, qkv, pt, ot, wa, wf = r_.x, r_.qkv, r_.pt, r_.ot, r_.wa, r_.wf
    hf, acc, par = r_.hf, r_.acc, r_.par
    seg_len, width = x.shape[1], x.shape[2]
    hidden = r_.u.shape[2]
    heads = pt.shape[1]
    local = ot.shape[2]
    hid = r_.w_back.shape[0]
    lanes = r_.norm_gains.shape[1]
    mem_rows = r_.memory_in.shape[0]
    text_rows = r_.text.shape[1]
    per_block = local // HD
    step = seg_len // head_count
    piece = step // 2
    chunk = hidden // head_count
    tail = 16
    tail_at = pl.ds(seg_len - tail, tail)

    def rows(r):
        return pl.ds(pl.multiple_of(r * step, step), step)

    def cols(i):
        return pl.ds(pl.multiple_of(i * chunk, chunk), chunk)

    def head_rows(h, part):
        return pl.ds(pl.multiple_of((h % per_block) * HD + part * local, HD), HD)

    def column(i):
        h = core if i < head_count - 1 else 1 - core
        zt = (z + 1 + i) % head_count
        return (plane * 2 + h) * head_count + zt, device(h, px, py, zt)

    column_size = 2 * head_count - 1

    def when_not(cond, body):
        pl.when(jnp.logical_not(cond))(body)

    share = local
    half = share // 2

    def attention_out(i, which):
        zt = (z + 1 + i) % head_count
        at = pl.multiple_of((share * jnp.minimum(plane, planes - 2) if which == 0 else 0) + half * core, half)
        src = (r_.wq_t, r_.w_out)[which]
        return push(
            src.at[pl.ds(at, half)], wa.at[z % 2, pl.ds(pl.multiple_of(share * plane + half * core, half), half)],
            r_.att_s.at[i], r_.att_r.at[z % 2, core], device(z // 2, px, py, zt),
        )

    def attention_outs(do):
        for which, mine in enumerate((plane < planes - 1, plane == planes - 1)):

            def each():
                for i in range(head_count - 1):
                    do(attention_out(i, which))

            pl.when(mine)(each)

    def attention_in(k, h):
        span = pl.ds(pl.multiple_of(share * plane + half * h, half), half)
        return push(r_.w_out.at[pl.ds(0, half)], wa.at[k, span], r_.att_s.at[0], r_.att_r.at[k, h], sibling)

    def attention_plane(k, which):
        at, count, mate = (
            (share * plane, share, x_mate),
            (share * plane, share, y_mate),
            (share * x_plane, half, y_mate),
            (share * y_plane + half, half, x_mate),
        )[which]
        block = pl.ds(pl.multiple_of(at, half), count)
        return push(
            wa.at[k, block], wa.at[k, block], r_.plane_s.at[k, which], r_.plane_r.at[k, which], mate
        )

    own_attention = [
        pltpu.make_async_copy(r_.wq_t, wa.at[z % 2, pl.ds(0, 3 * local)], r_.local_sem.at[0]),
        pltpu.make_async_copy(r_.w_out, wa.at[z % 2, pl.ds(3 * local, local)], r_.local_sem.at[1]),
    ]
    foreign = [jnp.logical_not(is_home & (z % 2 == k)) for k in range(2)]

    def rows_src(a, j, h):
        src = r_.text_pad if a < 2 else r_.cotangent
        return src.at[j, a % 2, pl.ds(h * piece, piece)]

    def rows_dst(a, zs, h):
        dst = r_.text_all if a < 2 else r_.cot_all
        return dst.at[a % 2, pl.ds(pl.multiple_of(zs * step + h * piece, piece), piece)]

    def rows_out(a, j, h):
        return push(
            rows_src(a, j, h), rows_dst(a, z, h), r_.rows_s.at[a, j, h], r_.rows_r.at[a, z],
            device(h, px, py, 2 * core + j),
        )

    def rows_here(a, j, h):
        return pltpu.make_async_copy(rows_src(a, j, h), rows_dst(a, z, h), r_.here_sem.at[a])

    def rows_send(a):
        for j in range(2):
            for h in range(2):
                here = (core == h) & (z == 2 * core + j)
                pl.when(here)(lambda: rows_here(a, j, h).start())
                when_not(here, lambda: rows_out(a, j, h).start())

    def rows_forward(a, zs, h):
        ref = rows_dst(a, zs, h)
        return push(ref, ref, r_.fwd_s.at[a, zs], r_.fwd_r.at[a, zs], sibling)

    def rows_pass(a):
        for zs in range(head_count):
            here = is_home & (z == zs)
            pl.when(here)(lambda: rows_here(a, z % 2, core).wait())
            when_not(
                here,
                lambda: push(
                    rows_src(a, 0, 0), rows_dst(a, zs, core), r_.rows_s.at[a, 0, 0], r_.rows_r.at[a, zs], sibling
                ).wait_recv(),
            )
            rows_forward(a, zs, core).start()

    def rows_ready(a):
        for zs in range(head_count):
            rows_forward(a, zs, 1 - core).wait_recv()

    def rows_done(a):
        for j in range(2):
            for h in range(2):
                when_not((core == h) & (z == 2 * core + j), lambda: rows_out(a, j, h).wait_send())
        for zs in range(head_count):
            rows_forward(a, zs, core).wait_send()

    def hidden_block(p, zi):
        return pl.ds(pl.multiple_of((zi * planes + p) * hid, hid), hid)

    def ffn_push(zi, to, slot):
        ref = wf.at[:, hidden_block(plane, zi)]
        return push(ref, ref, r_.ffn_s.at[slot], r_.ffn_r.at[zi], device(core, px, py, to))

    ffn_hops = [(0, from_end(1 - depth)), (0, from_end(2)), (1, from_end(2)), (2, from_end(0)), (3, from_end(0))]

    def ffn_hop(i):
        which, to = ffn_hops[i]
        return ffn_push(order[which], to, i)

    def ffn_own():
        ffn_hop(0).start()
        pl.when(inside)(ffn_hop(1).start)

    def ffn_hop_on(n):
        ffn_push(order[n], z, 0).wait_recv()
        pl.when(inside)(ffn_hop(n + 1).start)

    def ffn_sent():
        ffn_hop(0).wait_send()

        def rest():
            for i in range(1, 5):
                ffn_hop(i).wait_send()

        pl.when(inside)(rest)

    def side(kind, zi, which):
        p, mate = (
            (plane, x_mate),
            (plane, y_mate),
            (x_plane, y_mate) if kind == 0 else (y_plane, x_mate),
        )[which]
        ref = wf.at[kind, hidden_block(p, zi)]
        return push(ref, ref, r_.side_s.at[zi, kind, which], r_.side_r.at[zi, kind, which], mate)

    def side_first(zi):
        for kind in range(2):
            side(kind, zi, 0).start()
            side(kind, zi, 1).start()

    def ffn_two(n):
        zi = order_at(n)
        side(0, zi, 0).wait_recv()
        side(0, zi, 2).start()
        side(1, zi, 1).wait_recv()
        side(1, zi, 2).start()

    def ffn_ready(n):
        zi = order_at(n)
        side(0, zi, 1).wait_recv()
        side(1, zi, 0).wait_recv()
        side(0, zi, 2).wait_recv()
        side(1, zi, 2).wait_recv()

    def small_out(i):
        return push(r_.small, r_.small_all.at[me], r_.small_s.at[i], r_.small_r.at[z, core], column(i)[1])

    def small_in(i):
        at, (dp_i, z_i) = column(i)
        return push(r_.small, r_.small_all.at[at], r_.small_s.at[i], r_.small_r.at[z_i, dp_i % 2], sibling)

    def small_plane(i):
        p, mate = ((plane, x_mate), (plane, y_mate), (x_plane, y_mate))[i]
        ref = r_.small_all.at[pl.ds(p * 2 * head_count, 2 * head_count)]
        return push(ref, ref, r_.small_ps.at[i], r_.small_pr.at[i], mate)

    pair = [
        push(r_.seqf, r_.seqf_in, r_.pair_s.at[0], r_.pair_r.at[0], sibling),
        push(r_.memp, r_.memp_in, r_.pair_s.at[1], r_.pair_r.at[1], sibling),
    ]

    barrier = pltpu.get_barrier_semaphore()
    mates = [x_mate, y_mate] + [column(i)[1] for i in range(column_size)]
    for mate in mates:
        pl.semaphore_signal(barrier, inc=1, device_id=mate, device_id_type=MESH)
    wf[0, hidden_block(plane, z), :] = r_.w_in_t[...]
    wf[1, hidden_block(plane, z), :] = r_.w_back[...]
    vtmp = r_.vtmp
    vtmp[...] = jnp.zeros_like(vtmp)
    vtmp[0:2, 0:lanes] = r_.norm_gains[...].astype(F32)
    vtmp[2:6, 0:lanes] = r_.biases[...].astype(F32)
    vtmp[6 : 6 + mem_rows, 0:lanes] = r_.init_memory[...].astype(F32)
    vtmp[0:1, 32 : 32 + hid] = r_.b_in[...].astype(F32)
    for b in range(per_block):
        pair_b = r_.b_qv[b].astype(F32)
        for part in range(2):
            vtmp[1 + part * per_block + b : 2 + part * per_block + b, 32 : 32 + HD] = pair_b[part : part + 1, :]
    r_.small[...] = vtmp[...].astype(BF)
    r_.small_all[me] = r_.small[...]
    pl.semaphore_wait(barrier, len(mates))

    for i in range(column_size):
        small_out(i).start()
    side_first(z)
    ffn_own()
    attention_outs(lambda c: c.start())

    def keep_own():
        for copy in own_attention:
            copy.start()

    pl.when(is_home)(keep_own)
    seqf = r_.seqf
    marks = r_.boundary[z % 2].astype(F32).astype(BF)
    text_len = marks.shape[1]
    n_from = lax.broadcasted_iota(jnp.int32, (text_len, seg_len), 0)
    n_to = lax.broadcasted_iota(jnp.int32, (text_len, seg_len), 1) - mem_rows
    counts = nn(marks, jnp.where(n_from <= n_to, 1.0, 0.0).astype(BF))
    at_row = lax.broadcasted_iota(jnp.int32, (2, seg_len), 1)
    seqf[...] = jnp.zeros_like(seqf)
    seqf[0:2, :] = jnp.where((at_row >= mem_rows) & (at_row < seg_len - mem_rows), counts, -1.0)
    for s in range(2):
        seqf[2 + s : 3 + s, :] = jnp.full((1, seg_len), r_.reset[z % 2, s].astype(F32))
    r_.memp[...] = jnp.zeros_like(r_.memp)
    both_in = r_.memory_in[...].astype(F32)
    r_.memp[0:mem_rows, :] = jnp.where(z % 2 == 0, both_in[:, 0, :], both_in[:, 1, :]).astype(BF)
    for copy in pair:
        copy.start()

    def pad_text(j):
        both = r_.text[j].astype(F32)
        for s in range(2):
            r_.text_pad[j, s, 0:text_rows, :] = both[:, s, :].astype(BF)
            r_.text_pad[j, s, text_rows:step, :] = jnp.zeros((step - text_rows, width), BF)

    loop(2, pad_text)
    for ref in (r_.sg, r_.dinit, r_.dbin, r_.carry, r_.rs):
        ref[...] = jnp.zeros_like(ref)

    def attention_to_plane(k):
        for h in range(2):
            attention_in(k, h).wait_recv()
        attention_plane(k, 0).start()
        attention_plane(k, 1).start()

    def attention_across(k):
        attention_plane(k, 0).wait_recv()
        attention_plane(k, 2).start()
        attention_plane(k, 1).wait_recv()
        attention_plane(k, 3).start()

    for i in range(column_size):
        small_in(i).wait_recv()
    small_plane(0).start()
    small_plane(1).start()
    ffn_two(0)
    ffn_hop_on(1)
    pl.when(inside)(lambda: ffn_hop_on(2))
    side_first(order[1])
    rows_send(0)
    small_plane(0).wait_recv()
    small_plane(2).start()
    for k in range(2):
        pl.when(foreign[k] & is_home)(lambda: attention_to_plane(k))
    ffn_two(1)
    for k in range(2):
        pl.when(foreign[k] & away)(lambda: attention_to_plane(k))

    for copy in pair:
        copy.wait_recv()
    small_plane(1).wait_recv()
    small_plane(2).wait_recv()
    for i in range(total):
        par[0:16, lanes * i : lanes * (i + 1)] = r_.small_all[i, 0:16, 0:lanes].astype(F32)
    for zi in range(head_count):
        for p in range(planes):
            at = (zi * planes + p) * hid
            line = r_.small_all[(2 * p + core) * head_count + zi].astype(F32)
            r_.bin_row[0:1, at : at + hid] = line[0:1, 32 : 32 + hid]
    r_.bqv[...] = jnp.zeros_like(r_.bqv)
    for k in range(2):
        lines = r_.small_all[2 * core + k].astype(F32)
        for part in range(2):
            for b in range(per_block):
                line = lines[1 + part * per_block + b : 2 + part * per_block + b, 32 : 32 + HD]
                at = 2 * part * local + b * HD
                r_.bqv[k, at : at + HD, :] = as_column(line)
    seq = jnp.where(is_home, seqf[...], r_.seqf_in[...])
    seqf_out = r_.seq
    seqf_out[...] = seq
    flags = [seqf_out[2 + s : 3 + s, 0:1] for s in range(2)]
    tail_row = lax.broadcasted_iota(jnp.int32, (tail, width), 0)
    is_mem = tail_row >= tail - mem_rows
    init_b = jnp.where(is_mem, par[...], 0.0)
    given = jnp.where(is_home, r_.memp[...].astype(F32), r_.memp_in[...].astype(F32))
    first_b = jnp.where(flags[0] > 0, init_b, pltpu.roll(given, tail - mem_rows, 0))
    r_.cur_b[...] = first_b.astype(BF)
    r_.cur_a[...] = pltpu.roll(first_b, mem_rows, 0).astype(BF)

    def take_rows(r):
        inside = lax.broadcasted_iota(jnp.int32, (step, seg_len), 0)
        nat = lax.broadcasted_iota(jnp.int32, (step, seg_len), 1)
        return jnp.where((nat == r * text_rows + inside + mem_rows) & (inside < text_rows), 1.0, 0.0).astype(BF)

    def place_rows(r):
        nat = lax.broadcasted_iota(jnp.int32, (step, seg_len), 0) + r * step
        pad = lax.broadcasted_iota(jnp.int32, (step, seg_len), 1)
        inside = pad & (step - 1)
        target = (pad // step) * text_rows + inside + mem_rows
        return jnp.where((nat == target) & (inside < text_rows), 1.0, 0.0).astype(BF)

    wide = 2 * step

    def half_span(i):
        return pl.ds(pl.multiple_of(i * wide, wide), wide), i

    def end_span(i):
        return pl.ds(pl.multiple_of(i * (seg_len - step), step), step), i

    def middle_span(i):
        return pl.ds(step, wide), 2

    def exchange(slot, span):
        at, n = span
        return push(
            r_.send_buf.at[slot, at], r_.recv_buf.at[slot, at], r_.send_sem.at[slot, n], r_.recv_sem.at[slot, n],
            sibling,
        )

    def give(slot, span, part):
        at = span[0]
        acc[at, :] = part
        r_.send_buf[slot, at, :] = part.astype(BF)
        exchange(slot, span).start()

    def taken(slot, at):
        return acc[at, :] + r_.recv_buf[slot, at, :].astype(F32)

    def by_half(slot, body):
        def one(r):
            pl.when(r % 2 == 0)(lambda: exchange(slot, half_span(r // 2)).wait())
            body(rows(r))

        loop(head_count, one)

    def keep_scale(first, seg, at, scale):
        pair_at = slice(2 * first, 2 * first + 2)
        lane = lax.broadcasted_iota(jnp.int32, (1, 2), 1)
        r_.rs[at, pair_at] = jnp.where(lane == seg, scale, r_.rs[at, pair_at])

    def kept_scale(first, seg, at):
        lane = lax.broadcasted_iota(jnp.int32, (1, 2), 1)
        both = r_.rs[at, 2 * first : 2 * first + 2]
        return jnp.sum(jnp.where(lane == seg, both, 0.0), axis=1, keepdims=True)

    def back_copy(which, seg, zt):
        src, dst = ((r_.y, r_.acts_o), (r_.text_all, r_.text_pad))[which]
        span = pl.ds(pl.multiple_of(zt * step + core * piece, piece), piece)
        return src.at[seg, span], dst.at[z % 2, seg, pl.ds(core * piece, piece)]

    def back_out(which, seg, i):
        zt = (z + i) % head_count
        src, dst = back_copy(which, seg, zt)
        return push(
            src, dst, r_.back_s.at[which, seg, i], r_.back_r.at[which, seg, z % 2, core], device(z // 2, px, py, zt)
        )

    def back_here(which, seg):
        src, dst = back_copy(which, seg, z)
        return pltpu.make_async_copy(src, dst, r_.back_here_sem.at[which, seg])

    def back_send(which, seg):
        pl.when(is_home)(lambda: back_here(which, seg).start())
        pl.when(away)(lambda: back_out(which, seg, 0).start())
        for i in range(1, head_count):
            back_out(which, seg, i).start()

    def back_sent(which, seg):
        pl.when(is_home)(lambda: back_here(which, seg).wait())
        pl.when(away)(lambda: back_out(which, seg, 0).wait_send())
        for i in range(1, head_count):
            back_out(which, seg, i).wait_send()

    def back_done(which, seg):
        dst = (r_.acts_o, r_.text_pad)[which]
        for j in range(2):
            for h in range(2):
                when_not(
                    (core == h) & (z == 2 * core + j),
                    lambda: push(
                        r_.text_all.at[seg, pl.ds(0, piece)], dst.at[j, seg, pl.ds(h * piece, piece)],
                        r_.back_s.at[which, seg, 0], r_.back_r.at[which, seg, j, h], sibling,
                    ).wait_recv(),
                )

    def tail_z(which, i):
        zt = (z + 1 + i) % head_count
        to = device(core, px, py, zt)
        dst = r_.factors.at[which, z, plane]
        return push(r_.factor_out.at[which, zt], dst, r_.tg_s.at[which, i], r_.tg_r.at[which, z], to)

    def tail_z_in(which, i):
        zs = (z + 1 + i) % head_count
        dst = r_.factors.at[which, zs, plane]
        return push(r_.factor_out.at[which, zs], dst, r_.tg_s.at[which, i], r_.tg_r.at[which, zs], sibling)

    def tail_plane(which, i):
        p, zs, to = (
            (plane, slice(None), x_mate), (plane, slice(None), y_mate),
            (x_plane, pl.ds(0, 2), y_mate), (y_plane, pl.ds(2, 2), x_mate),
        )[i]
        buf = r_.factors.at[which, zs, p]
        return push(buf, buf, r_.tg_s.at[which, 3 + i], r_.tg_r.at[which, head_count + i], to)

    def tail_pair(which):
        src = r_.factors.at[which, :, :, :, pl.ds(0, half_width)]
        return push(src, r_.factors_in.at[which], r_.tp_s.at[which], r_.tp_r.at[which], sibling)

    def tail_gather(which, stage):
        if stage == 0:
            for i in range(head_count - 1):
                tail_z(which, i).start()
            r_.factors[which, z, plane] = r_.factor_out[which, z]
        elif stage == 1:
            for i in range(head_count - 1):
                tail_z_in(which, i).wait_recv()
            tail_plane(which, 0).start()
            tail_plane(which, 1).start()
        elif stage == 2:
            for i in range(2):
                tail_plane(which, i).wait_recv()
                tail_plane(which, 2 + i).start()
        elif stage == 3:
            for i in range(2):
                tail_plane(which, 2 + i).wait_recv()
            tail_pair(which).start()
        else:
            for i in range(head_count - 1):
                tail_z(which, i).wait_send()
            for i in range(4):
                tail_plane(which, i).wait_send()

    half_width = width // 2

    def half_of(h):
        return pl.ds(pl.multiple_of(h * half_width, half_width), half_width)

    def tail_put(which, hidden_ref, units):
        part = hidden_ref[0, tail_at, half_of(core)]
        for zt in range(head_count):
            r_.factor_out[which, zt, :, 0:half_width] = part
            r_.factor_out[which, zt, :, half_width:] = units[:, zt * chunk : (zt + 1) * chunk]
        tail_gather(which, 0)

    def tail_products():
        down = lax.broadcasted_iota(jnp.int32, (chunk, 128), 0)
        across = lax.broadcasted_iota(jnp.int32, (chunk, 128), 1)
        pick = jnp.where((down == plane * hid + across) & (across < hid), 1.0, 0.0).astype(BF)
        all_rows = planes * head_count * tail
        units = [
            nn(r_.factors[which, :, :, :, half_width:].reshape(all_rows, chunk), pick).astype(BF) for which in range(2)
        ]
        for which in range(2):
            tail_pair(which).wait()
        out = []
        for kind in range(2):
            mine = tn(units[1 - kind], r_.factors[kind, :, :, :, 0:half_width].reshape(all_rows, half_width))[0:hid, :]
            theirs = tn(units[1 - kind], r_.factors_in[kind].reshape(all_rows, half_width))[0:hid, :]
            out.append((mine, theirs))
        return out

    def build(seg):
        def one(r):
            x[seg, rows(r), :] = nn(place_rows(r), r_.text_all[seg]).astype(BF)

        loop(head_count, one)

    def add_memory(seg):
        x[seg, 0:tail, :] = x[seg, 0:tail, :] + r_.cur_a[...]
        x[seg, tail_at, :] = x[seg, tail_at, :] + r_.cur_b[...]

    def make_mask(seg):
        right = r_.seq[pl.ds(seg, 1), :]
        left = as_column(right)
        acc[:, 0:seg_len] = jnp.where((left == right) | (left < 0) | (right < 0), 0.0, -1e30)

    def keep_projected(seg, j, at, value):
        value = value + r_.bqv[j]
        qkv[seg, j, 0:local, at] = (value[0:local, :] * 0.125).astype(BF)
        qkv[seg, j, local:, at] = value[local:, :].astype(BF)

    def project(seg):
        def one(j):
            keep_projected(seg, j, slice(None), nt(wa[j, 0 : 3 * local, :], x[seg]))

        loop(2, one)

    def project_ends(seg):
        both = jnp.concatenate([x[seg, 0:step, :], x[seg, seg_len - step :, :]], axis=0)

        def one(j):
            value = nt(wa[j, 0 : 3 * local, :], both)
            keep_projected(seg, j, slice(0, step), value[:, 0:step])
            keep_projected(seg, j, slice(seg_len - step, seg_len), value[:, step:])

        loop(2, one)

    def attend(seg):
        def one(h):
            j = h // per_block
            q, k, v = (qkv[seg, j, head_rows(h, part), :] for part in range(3))
            s = tn(k, q) + acc[:, 0:seg_len]
            e = jnp.exp(s - jnp.max(s, axis=0, keepdims=True))
            p = (e * (1.0 / jnp.sum(e, axis=0, keepdims=True))).astype(BF)
            pt[seg, h] = p
            ot[seg, j, head_rows(h, 0), :] = nn(v, p).astype(BF)

        loop(heads, one, unroll=2)

    def out_project(seg):
        def one(i):
            span = half_span(i)
            at = span[0]
            give(
                0, span, tn(ot[seg, 0, :, at], wa[0, 3 * local :, :]) + tn(ot[seg, 1, :, at], wa[1, 3 * local :, :])
            )

        loop(2, one)

    def norm_one(seg):
        def one(at):
            hat, scale = norm(x[seg, at, :].astype(F32) + taken(0, at) + par[3:4, :])
            r_.xh1[seg, at, :] = hat.astype(BF)
            keep_scale(0, seg, at, scale)
            h = hat * par[0:1, :] + par[2:3, :]
            hf[at, :] = h
            r_.hb[seg, at, :] = h.astype(BF)

        by_half(0, one)

    def inner(seg, at):
        v = nt(r_.hb[seg], wf[0, at, :]) + r_.bin_row[:, at]
        c0 = 0.7978845608028654
        sq = v * v
        th = jnp.tanh(v * (c0 + (c0 * 0.044715) * sq))
        up = 0.5 + 0.5 * th
        active = v * up
        r_.u[seg, :, at] = active.astype(BF)
        slope = up + active * (1.0 - up) * (2 * c0 + (6 * c0 * 0.044715) * sq)
        r_.gp[seg, :, at] = slope.astype(BF)

    def outer(seg):
        def one(i):
            span = half_span(i)
            give(1, span, nn(r_.u[seg, span[0], :], wf[1]))

        loop(2, one)

    def norm_two(seg):
        def one(at):
            hat, scale = norm(hf[at, :] + taken(1, at) + par[4:5, :])
            r_.xh2[seg, at, :] = hat.astype(BF)
            keep_scale(1, seg, at, scale)
            r_.y[seg, at, :] = (hat * par[1:2, :] + par[5:6, :]).astype(BF)

        by_half(1, one)

    def next_memory():
        last = r_.y[0, tail_at, :].astype(F32)
        memory = jnp.where(is_mem, jnp.where(flags[1] > 0, par[...], last), 0.0)
        r_.cur_b[...] = memory.astype(BF)
        r_.cur_a[...] = pltpu.roll(memory, mem_rows, 0).astype(BF)

    pl.when(inside)(lambda: ffn_hop_on(3))
    pl.when(depth == 0)(lambda: ffn_hop_on(2))
    for k in range(2):
        pl.when(foreign[k])(lambda: attention_across(k))
    side_first(order[2])
    rows_pass(0)
    rows_ready(0)
    build(0)
    add_memory(0)
    for k in range(2):

        def last_part():
            attention_plane(k, 2).wait_recv()
            attention_plane(k, 3).wait_recv()

        pl.when(foreign[k])(last_part)

    def kept_own():
        for copy in own_attention:
            copy.wait()

    pl.when(is_home)(kept_own)
    project(0)
    pl.when(depth == 0)(lambda: ffn_hop_on(3))
    side_first(order[3])
    rows_send(1)

    def forward(seg):
        make_mask(seg)
        attend(seg)

        def between():
            rows_pass(3)
            back_send(0, 0)

        pl.when(seg == 1)(between)
        out_project(seg)

        def rows_next():
            ffn_two(2)
            rows_send(3)
            rows_send(2)

        pl.when(seg == 0)(rows_next)
        norm_one(seg)

        def units(n):
            def start_two():
                ffn_two(3)
                rows_ready(1)
                build(1)
                project(1)

            def rows_on():
                rows_pass(1)

            pl.when(n == 2)(rows_on)
            pl.when(n == 3)(start_two)
            ffn_ready(n)
            inner(0, cols(order_at(n)))

        def wide_units():
            loop(2, lambda n: inner(1, pl.ds(pl.multiple_of(n * 2 * chunk, 2 * chunk), 2 * chunk)))

        pl.when(seg == 0)(lambda: loop(head_count, units))
        pl.when(seg == 1)(wide_units)
        outer(seg)
        pl.when(seg == 1)(lambda: rows_pass(2))
        norm_two(seg)

        def on_to_two():
            rows_done(0)
            rows_done(1)
            next_memory()
            add_memory(1)
            project_ends(1)
            tail_put(0, r_.hb, r_.u[0, tail_at, :])

        pl.when(seg == 0)(on_to_two)

    loop(2, forward)
    back_send(0, 1)
    rows_ready(3)

    def pull_two_part(g_y, hat, scale):
        pre = pull_norm(g_y * par[1:2, :], hat, scale)
        r_.sg[1:2, :] += row_sum(g_y * hat)
        r_.sg[5:6, :] += row_sum(g_y)
        r_.sg[4:5, :] += row_sum(pre)
        return pre.astype(BF)

    def pull_two():
        def one(n):
            seg, r = 1 - n // head_count, n % head_count
            pl.when(n == head_count)(lambda: rows_ready(2))
            below = lax.broadcasted_iota(jnp.int32, (step, width), 0) + r * step
            held = (below >= seg_len - tail) & (seg == 0)
            g_y = jnp.where(held, 0.0, r_.cot_all[seg, rows(r), :].astype(F32))
            hat = r_.xh2[seg, rows(r), :].astype(F32)
            r_.xh2[seg, rows(r), :] = pull_two_part(g_y, hat, kept_scale(1, seg, rows(r)))

        loop(2 * head_count, one)

    def keep_tail():
        r_.xh2_t[...] = r_.xh2[0, tail_at, :]
        r_.gp_t[...] = r_.gp[0, tail_at, :]

    def pull_tail():
        g_y = r_.cot_all[0, tail_at, :].astype(F32) + r_.carry[...]
        pre = pull_two_part(g_y, r_.xh2_t[...].astype(F32), kept_scale(1, 0, tail_at))
        r_.xh2[0, tail_at, :] = pre
        g_z = (nt(pre, wf[1]) * r_.gp_t[...].astype(F32)).astype(BF)
        r_.gp[0, tail_at, :] = g_z
        r_.dbin[0:1, :] += row_sum(g_z.astype(F32))
        tail_put(1, r_.xh2, g_z)

    def pull_inner(i):
        both = r_.xh2[...].reshape(2 * seg_len, width)
        g_u = nt(both, wf[1, cols(i), :])
        for seg in range(2):
            g_z = (g_u[seg * seg_len : (seg + 1) * seg_len, :] * r_.gp[seg, :, cols(i)].astype(F32)).astype(BF)
            r_.gp[seg, :, cols(i)] = g_z
            r_.dbin[0:1, cols(i)] += row_sum(g_z.astype(F32))

    def pull_hidden(seg):
        def one(i):
            span = half_span(i)
            give(0, span, nn(r_.gp[seg, span[0], :], wf[0]))

        loop(2, one)

    def pull_one(seg):
        def one(at):
            g_h = r_.xh2[seg, at, :].astype(F32) + taken(0, at)
            hat = r_.xh1[seg, at, :].astype(F32)
            pre = pull_norm(g_h * par[0:1, :], hat, kept_scale(0, seg, at))
            hf[at, :] = pre
            r_.xh1[seg, at, :] = pre.astype(BF)
            r_.sg[0:1, :] += row_sum(g_h * hat)
            r_.sg[2:3, :] += row_sum(g_h)
            r_.sg[3:4, :] += row_sum(pre)

        by_half(0, one)

        def out(j):
            r_.got[j] = nt(wa[j, 3 * local :, :], r_.xh1[seg]).astype(BF)

        loop(2, out)

    def pull_heads(seg):
        def one(h):
            j = h // per_block
            q, k, v = (qkv[seg, j, head_rows(h, part), :] for part in range(3))
            g_o = r_.got[j, head_rows(h, 0), :]
            p = pt[seg, h]
            d_v = nt(g_o, p).astype(BF)
            total_p = row_sum(g_o.astype(F32) * ot[seg, j, head_rows(h, 0), :].astype(F32))
            d_s = (p.astype(F32) * (tn(v, g_o) - total_p)).astype(BF)
            d_q = (nn(k, d_s) * 0.125).astype(BF)
            d_k = nt(q, d_s).astype(BF)
            for part, value in enumerate((d_q, d_k, d_v)):
                qkv[seg, j, head_rows(h, part), :] = value

        loop(heads, one, unroll=2)

    def pull_rows(seg, span):
        at = span[0]
        give(
            1, span,
            tn(qkv[seg, 0, :, at], wa[0, 0 : 3 * local, :]) + tn(qkv[seg, 1, :, at], wa[1, 0 : 3 * local, :]),
        )

    def pull_x(at):
        value = hf[at, :] + taken(1, at)
        acc[at, :] = value
        r_.send_buf[1, at, :] = value.astype(BF)

    def pull_memory(seg):
        both = pltpu.roll(acc[0:tail, :], tail - mem_rows, 0) + acc[seg_len - tail : seg_len, :]
        memory = jnp.where(is_mem, both, 0.0)
        r_.dinit[...] += jnp.where(flags[seg] > 0, memory, 0.0)
        if seg == 1:
            r_.carry[...] = jnp.where(flags[1] > 0, 0.0, memory)

    def text_grad(seg):
        def one(r):
            r_.text_all[seg, rows(r), :] = nn(take_rows(r), r_.send_buf[1]).astype(BF)

        loop(head_count, one)

    def cut(buf, kind, a, b):
        first, second = (px, py) if kind == 0 else (py, px)
        first = first if a == 0 else 1 - first
        second = second if b == 0 else 1 - second
        return buf.at[second, first] if kind == 0 else buf.at[first, second]

    def parts_of(name):
        return sums[name] if isinstance(name, str) else ffn_sum(name)

    sum_mates = ((x_mate, y_mate), (y_mate, x_mate))

    def sum_one(name, kind, b):
        buf, got, s, r = parts_of(name)(kind)
        return push(cut(buf, kind, 1, b), got[0].at[b], s.at[b], r.at[b], sum_mates[kind][0])

    def sum_two(name, kind):
        buf, got, s, r = parts_of(name)(kind)
        return push(cut(buf, kind, 0, 1), got[1], s.at[2], r.at[2], sum_mates[kind][1])

    def ffn_sum(d):
        zi = order_at(d)

        def parts(kind):
            return (
                r_.fsend.at[kind, zi], (r_.f_one.at[kind, zi], r_.f_two.at[kind, zi]),
                r_.fsum_s.at[kind, zi], r_.fsum_r.at[kind, zi],
            )

        return parts

    sums = {}

    def attention_sum(n):
        def parts(kind):
            return (
                r_.asend.at[n, kind], (r_.a_one.at[n, kind], r_.a_two.at[n, kind]),
                r_.asum_s.at[n, kind], r_.asum_r.at[n, kind],
            )

        return parts

    halves = ("a", "b")
    for n, name in enumerate(halves):
        sums[name] = attention_sum(n)
    sums["v"] = lambda kind: (
        r_.vsend.at[kind], (r_.v_one.at[kind], r_.v_two.at[kind]), r_.vsum_s.at[kind], r_.vsum_r.at[kind]
    )

    def start_sum(name, which=((1, 0), (1, 1), (0, 0), (0, 1))):
        for b, kind in which:
            sum_one(name, kind, b).start()

    def travel(name):
        for kind in range(2):
            buf, got, _, _ = parts_of(name)(kind)
            sum_one(name, kind, 1).wait_recv()
            add_all(cut(buf, kind, 0, 1), got[0].at[1])
            sum_two(name, kind).start()

    def end_plane(name):
        for kind in range(2):
            buf, got, _, _ = parts_of(name)(kind)
            sum_one(name, kind, 0).wait_recv()
            sum_two(name, kind).wait_recv()
            add_all(cut(buf, kind, 0, 0), got[0].at[0], got[1])

    def sum_sent(name):
        for kind in range(2):
            for b in range(2):
                sum_one(name, kind, b).wait_send()
            sum_two(name, kind).wait_send()

    def z_out(kind, d):
        slot = jnp.where(inside, jnp.where(d == 1, 0, jnp.where(d == 2, 4, 1)), jnp.where(d == 1, 0, d))
        to = from_end(jnp.where(inside, jnp.where(d == 1, 0, 2), 1))
        return push(
            cut(r_.fsend.at[kind, order_at(d)], kind, 0, 0), r_.f_z.at[kind, slot], r_.fz_s.at[kind, d],
            r_.fz_r.at[kind, slot], device(core, px, py, to),
        )

    def z_in(kind, slot):
        return push(
            cut(r_.fsend.at[kind, z], kind, 0, 0), r_.f_z.at[kind, slot], r_.fz_s.at[kind, 0], r_.fz_r.at[kind, slot],
            sibling,
        )

    def end_ffn(d):
        end_plane(d)

        def send():
            for kind in range(2):
                z_out(kind, d).start()

        if d > 0:
            pl.when(depth == 0)(send)

    def z_pass(d):
        def add_and_send():
            for kind in range(2):
                z_in(kind, d).wait_recv()
                add_all(cut(r_.fsend.at[kind, order_at(d)], kind, 0, 0), r_.f_z.at[kind, d])
                z_out(kind, d).start()

        pl.when(inside)(add_and_send)

    def last_out(name, k, h):
        buf, dst, s, r = last[name]
        return push(
            cut(buf.at[k], k, 0, 0).at[h], dst.at[z], s.at[k, h], r.at[z], device(h, px, py, 2 * core + k)
        )

    def last_here(name, k):
        buf, dst, _, _ = last[name]
        return pltpu.make_async_copy(cut(buf.at[k], k, 0, 0).at[core], dst.at[z], r_.last_sem.at["abv".index(name)])

    last = {
        "a": (r_.asend.at[0], r_.a_z.at[0], r_.az_s.at[0], r_.az_r.at[0]),
        "b": (r_.asend.at[1], r_.a_z.at[1], r_.az_s.at[1], r_.az_r.at[1]),
        "v": (r_.vsend, r_.v_z, r_.vz_s, r_.vz_r),
    }

    def last_each(name, here_do, away_do):
        for k in range(2):
            for h in range(2):
                here = (core == h) & (z == 2 * core + k)
                if here_do is not None:
                    pl.when(here)(lambda: here_do(last_here(name, k)))
                when_not(here, lambda: away_do(last_out(name, k, h)))

    def last_total(name):
        buf, dst, s, r = last[name]
        for zs in range(head_count):
            here = is_home & (z == zs)
            pl.when(here)(lambda: last_here(name, 0).wait())
            when_not(
                here, lambda: push(buf.at[0, 0, 0, 0], dst.at[zs], s.at[0, 0], r.at[zs], sibling).wait_recv()
            )
        value = dst[0].astype(F32)
        for zs in range(1, head_count):
            value = value + dst[zs].astype(F32)
        return value

    def ffn_grads(d):
        i = order_at(d)

        def grads(kind, left, right):
            value = tn(left[0, :, cols(i)], right[0]) + tn(left[1, :, cols(i)], right[1])
            for p in range(planes):
                r_.fsend[kind, i, p // 2, p % 2] = value[p * hid : (p + 1) * hid, :].astype(BF)

        grads(1, r_.u, r_.xh2)

        def first_kind():
            pl.when(d == 2)(lambda: travel(3))
            start_sum(d, ((1, 1), (0, 1)))

        pl.when(d >= 2)(first_kind)
        pull_inner(i)
        grads(0, r_.gp, r_.hb)
        pl.when(d >= 2)(lambda: start_sum(d, ((1, 0), (0, 0))))

    keep_tail()
    pull_two()
    tail_gather(0, 1)
    loop(head_count, lambda n: ffn_grads(head_count - 1 - n))
    dbin_pair = push(r_.dbin, r_.dbin_in, r_.pair_s.at[2], r_.pair_r.at[2], sibling)

    def backward(n):
        seg = 1 - n
        pull_hidden(seg)

        pull_one(seg)

        def first_events():
            end_ffn(3)
            travel(2)
            start_sum(1)
            start_sum(0)
            tail_gather(0, 2)

        pl.when(seg == 1)(first_events)
        pull_heads(seg)

        def segment_two():
            loop(2, lambda i: pull_rows(1, end_span(i)))

            def one(i):
                exchange(1, end_span(i)).wait()
                pull_x(end_span(i)[0])

            loop(2, one)
            pull_memory(1)
            pull_tail()
            dbin_pair.start()
            pull_rows(1, middle_span(0))
            z_pass(3)
            end_ffn(2)
            travel(1)
            exchange(1, middle_span(0)).wait()
            pull_x(middle_span(0)[0])
            text_grad(1)
            back_send(1, 1)

        pl.when(seg == 1)(segment_two)

    loop(2, backward)
    travel(0)
    z_pass(2)
    hid_rows = width // dp_count
    cut_rows = hid_rows // 2

    def attention_grads(i):
        wide = width // 2
        span = pl.ds(pl.multiple_of(i * wide, wide), wide)
        xt = [x[s, :, span].T for s in range(2)]
        gt = [r_.xh1[s, :, span].T for s in range(2)]
        for k in range(2):
            qkv_g = nt(xt[0], qkv[0, k]) + nt(xt[1], qkv[1, k])
            out_g = nt(gt[0], ot[0, k]) + nt(gt[1], ot[1, k])
            for b in range(8):
                at = slice(b * cut_rows, (b + 1) * cut_rows)
                r_.asend[b % 2, k, i, b // 4, (b // 2) % 2, :, 0 : 3 * local] = qkv_g[at, :].astype(BF)
                r_.asend[b % 2, k, i, b // 4, (b // 2) % 2, :, 3 * local :] = out_g[at, :].astype(BF)

    def both_planes(n):
        attention_grads(jnp.where(n == 0, 1 - py, py))

        def travelling():
            for name in halves:
                start_sum(name, ((1, 0), (1, 1)))

        pl.when(n == 0)(travelling)

    loop(2, both_planes)
    start_sum("a", ((0, 1), (0, 0)))
    tail_gather(1, 1)
    end_ffn(1)
    loop(2, lambda i: pull_rows(0, half_span(i)))
    by_half(1, pull_x)
    pull_memory(0)
    dbin_pair.wait()

    dbin_both = [jnp.where(core == h, r_.dbin[0:1, :], r_.dbin_in[0:1, :]) for h in range(2)]
    for k in range(2):
        r_.bqv[k] = sum(jnp.sum(qkv[s, k].astype(F32), axis=1, keepdims=True) for s in range(2))
    sg, dinit = r_.sg, r_.dinit
    r_.vec[...] = jnp.where(is_mem, dinit[...], 0.0)
    r_.vec[0:6, :] = sg[0:6, :]
    vtmp[...] = jnp.zeros_like(vtmp)

    def by_core(cut_of):
        return jnp.where(core == 0, cut_of(0), cut_of(1))

    qv_rows = [
        [
            jnp.sum(
                jnp.where(
                    lax.broadcasted_iota(jnp.int32, (HD, HD), 0) == lax.broadcasted_iota(jnp.int32, (HD, HD), 1),
                    r_.bqv[k, 2 * part * local + b * HD : 2 * part * local + (b + 1) * HD, :],
                    0.0,
                ),
                axis=0,
                keepdims=True,
            )
            for part in range(2)
            for b in range(per_block)
        ]
        for k in range(2)
    ]
    piece_b = HD // dp_count
    vec = r_.vec[...]

    def small_cut(k, p, h):
        dp_t = 2 * p + h

        def from_vec(c):
            at = (dp_t * head_count + 2 * c + k) * lanes
            return vec[:, at : at + lanes]

        def from_bin(c):
            at = ((2 * c + k) * planes + p) * hid
            return dbin_both[h][:, at : at + hid]

        vtmp[0:16, 0:lanes] = by_core(from_vec)
        vtmp[0:1, 32 : 32 + hid] = by_core(from_bin)
        for n, line in enumerate(qv_rows[k]):
            vtmp[1:2, 32 + n * piece_b : 32 + (n + 1) * piece_b] = line[:, dp_t * piece_b : (dp_t + 1) * piece_b]
        r_.vsend[k, p // 2, p % 2, h] = vtmp[...].astype(BF)

    for k in range(2):
        for p in range(planes):
            for h in range(2):
                small_cut(k, p, h)
    start_sum("v")
    end_ffn(0)
    z_pass(1)
    travel("a")
    start_sum("b", ((0, 1), (0, 0)))
    text_grad(0)
    back_send(1, 0)
    travel("b")
    travel("v")
    end_plane("a")
    last_each("a", lambda c: c.start(), lambda c: c.start())
    tail_gather(1, 2)
    end_plane("v")
    last_each("v", lambda c: c.start(), lambda c: c.start())
    end_plane("b")
    last_each("b", lambda c: c.start(), lambda c: c.start())

    tail_gather(0, 3)
    tail_gather(1, 3)
    extra = tail_products()
    for kind, out in enumerate((r_.win_o, r_.wback_o)):
        value = cut(r_.fsend.at[kind, z], kind, 0, 0)[...].astype(F32)
        z_in(kind, 0).wait_recv()
        out[...] = value + r_.f_z[kind, 0].astype(F32)

        def other_side():
            z_in(kind, 4).wait_recv()
            out[...] += r_.f_z[kind, 4].astype(F32)

        pl.when(inside)(other_side)
        out[:, half_of(core)] += extra[kind][0]
        out[:, half_of(1 - core)] += extra[kind][1]


    for name in (0, 1, 2, 3, "a", "b", "v"):
        sum_sent(name)
    for d in range(1, head_count):
        for kind in range(2):
            z_out(kind, d).wait_send()
    for which in range(2):
        for seg in range(2):
            back_sent(which, seg)
            back_done(which, seg)
    for a in range(2, 4):
        rows_done(a)
    attention_outs(lambda c: c.wait_send())
    ffn_sent()
    for which in range(2):
        tail_gather(which, 4)
    for copy in pair:
        copy.wait_send()
    for k in range(2):

        def sent():
            for which in range(4):
                attention_plane(k, which).wait_send()

        pl.when(foreign[k])(sent)
    for zi in range(head_count):
        for kind in range(2):
            for which in range(3):
                side(kind, zi, which).wait_send()
    for i in range(column_size):
        small_out(i).wait_send()
    for i in range(3):
        small_plane(i).wait_send()
    for j in range(2):
        both = [r_.text_pad[j, s, 0:text_rows, :].astype(F32)[:, None, :] for s in range(2)]
        r_.dt_o[j] = jnp.concatenate(both, axis=1).astype(BF)
    r_.att_o[0:cut_rows, :] = last_total("a")
    r_.att_o[cut_rows:hid_rows, :] = last_total("b")
    r_.vec_o[...] = last_total("v")
    for name in "abv":
        last_each(name, None, lambda c: c.wait_send())


def vmem(*shape, dtype=BF):
    return pltpu.VMEM(shape, dtype)


def f32(*shape):
    return pltpu.VMEM(shape, F32)


def sds(*shape, dtype=BF):
    return jax.ShapeDtypeStruct(shape, dtype)


def dma(*shape):
    return pltpu.SemaphoreType.DMA(shape)


ANY = pl.BlockSpec(memory_space=pl.ANY)
INV = pl.BlockSpec(memory_space=pltpu.VMEM)
INS = pl.BlockSpec(memory_space=pltpu.SMEM)


def end_kernel(mem_rows, hid, lanes, acts, dt, win, wback, att, vec, *outs):
    acts_o, dt_o, dinit_o, dqkv_o, dbqv_o, dwout_o, dwin_o, dwback_o, dbin_o, dgains_o, dbiases_o = outs
    acts_o[...] = acts[...]
    dt_o[...] = dt[...]
    dinit_o[...] = vec[6 : 6 + mem_rows, 0:lanes]
    parts, _, local_width = dqkv_o.shape
    for t in range(parts):
        dqkv_o[t] = att[:, t * local_width : (t + 1) * local_width]
    per_block, _, slice_b = dbqv_o.shape
    for b in range(per_block):
        for part in range(2):
            at = 32 + (part * per_block + b) * slice_b
            dbqv_o[b, part : part + 1, :] = vec[1:2, at : at + slice_b]
    dwout_o[...] = att[:, parts * local_width :].T
    dwin_o[...] = win[...]
    dwback_o[...] = wback[...]
    dbin_o[...] = vec[0:1, 32 : 32 + hid]
    dgains_o[...] = vec[0:2, 0:lanes]
    dbiases_o[...] = vec[2:6, 0:lanes]


def by_chip(
    text, boundary, reset, memory_in, init_memory, w_qkv, b_qv, w_out, w_in, w_back, b_in, norm_gains, biases,
    cotangent,
):
    head_count = lax.axis_size("head")
    dp_count = lax.axis_size("dp")
    planes = dp_count // 2
    total = dp_count * head_count
    text_rows, width = text.shape[2], text.shape[3]
    block = cotangent.shape[2]
    seg_len = block * head_count
    mem_rows = memory_in.shape[1]
    local = w_qkv.shape[2]
    hid = w_in.shape[1]
    lanes = norm_gains.shape[1]
    heads = 2 * local // HD
    hidden = hid * planes * head_count
    share = width // dp_count

    inputs = dict(
        text=(text.transpose(0, 2, 1, 3), INV),
        boundary=(boundary, INV),
        reset=(reset, INS),
        memory_in=(memory_in.transpose(1, 0, 2), INV),
        init_memory=(init_memory, INV),
        wq_t=(w_qkv.transpose(1, 2, 0).reshape(3 * local, width), ANY),
        w_out=(w_out, ANY),
        b_qv=(b_qv.transpose(1, 0, 2), INV),
        w_in_t=(w_in.T, INV),
        w_back=(w_back, INV),
        b_in=(b_in[None, :], INV),
        norm_gains=(norm_gains, INV),
        biases=(biases, INV),
        cotangent=(cotangent, ANY),
    )
    outputs = dict(
        acts_o=(sds(2, 2, block, width), ANY),
        dt_o=(sds(2, text_rows, 2, width), INV),
        win_o=(sds(hid, width, dtype=F32), INV),
        wback_o=(sds(hid, width, dtype=F32), INV),
        att_o=(sds(share, width, dtype=F32), INV),
        vec_o=(sds(16, 128, dtype=F32), INV),
    )
    scratch = dict(
        text_pad=vmem(2, 2, block, width),
        text_all=vmem(2, seg_len, width),
        cot_all=vmem(2, seg_len, width),
        wa=vmem(2, 4 * local, width),
        wf=vmem(2, hidden, width),
        small=vmem(16, 128),
        small_all=vmem(total, 16, 128),
        seqf=f32(8, seg_len),
        seqf_in=f32(8, seg_len),
        seq=f32(8, seg_len),
        memp=vmem(16, width),
        memp_in=vmem(16, width),
        par=f32(16, width),
        bin_row=f32(1, hidden),
        bqv=f32(2, 3 * local, 1),
        x=vmem(2, seg_len, width),
        qkv=vmem(2, 2, 3 * local, seg_len),
        pt=vmem(2, heads, seg_len, seg_len),
        ot=vmem(2, 2, local, seg_len),
        hf=f32(seg_len, width),
        acc=f32(seg_len, width),
        xh1=vmem(2, seg_len, width),
        hb=vmem(2, seg_len, width),
        u=vmem(2, seg_len, hidden),
        gp=vmem(2, seg_len, hidden),
        xh2=vmem(2, seg_len, width),
        rs=f32(seg_len, 4),
        y=vmem(2, seg_len, width),
        got=vmem(2, local, seg_len),
        send_buf=vmem(2, seg_len, width),
        recv_buf=vmem(2, seg_len, width),
        cur_a=vmem(16, width),
        cur_b=vmem(16, width),
        carry=f32(16, width),
        xh2_t=vmem(16, width),
        gp_t=vmem(16, hidden),
        factor_out=vmem(2, head_count, 16, width // 2 + hidden // head_count),
        factors=vmem(2, head_count, planes, 16, width // 2 + hidden // head_count),
        factors_in=vmem(2, head_count, planes, 16, width // 2),
        sg=f32(8, width),
        dinit=f32(16, width),
        dbin=f32(8, hidden),
        dbin_in=f32(8, hidden),
        vec=f32(16, width),
        vtmp=f32(16, 128),
        fsend=vmem(2, head_count, 2, 2, hid, width),
        f_one=vmem(2, head_count, 2, hid, width),
        f_two=vmem(2, head_count, hid, width),
        f_z=vmem(2, head_count + 1, hid, width),
        asend=vmem(2, 2, 2, 2, 2, share // 2, width),
        a_one=vmem(2, 2, 2, 2, share // 2, width),
        a_two=vmem(2, 2, 2, share // 2, width),
        a_z=vmem(2, head_count, share // 2, width),
        vsend=vmem(2, 2, 2, 2, 16, 128),
        v_one=vmem(2, 2, 2, 16, 128),
        v_two=vmem(2, 2, 16, 128),
        v_z=vmem(head_count, 16, 128),
        small_s=dma(7),
        small_r=dma(4, 2),
        small_ps=dma(3),
        small_pr=dma(3),
        pair_s=dma(3),
        pair_r=dma(3),
        att_s=dma(3),
        att_r=dma(2, 2),
        plane_s=dma(2, 4),
        plane_r=dma(2, 4),
        local_sem=dma(2),
        rows_s=dma(4, 2, 2),
        rows_r=dma(4, 4),
        here_sem=dma(4),
        fwd_s=dma(4, 4),
        fwd_r=dma(4, 4),
        ffn_s=dma(5),
        ffn_r=dma(4),
        side_s=dma(4, 2, 3),
        side_r=dma(4, 2, 3),
        send_sem=dma(2, 4),
        recv_sem=dma(2, 4),
        back_s=dma(2, 2, 4),
        back_r=dma(2, 2, 2, 2),
        back_here_sem=dma(2, 2),
        fsum_s=dma(2, 4, 3),
        fsum_r=dma(2, 4, 3),
        asum_s=dma(2, 2, 3),
        asum_r=dma(2, 2, 3),
        tg_s=dma(2, 7),
        tg_r=dma(2, 8),
        tp_s=dma(2),
        tp_r=dma(2),
        vsum_s=dma(2, 3),
        vsum_r=dma(2, 3),
        fz_s=dma(2, 4),
        fz_r=dma(2, 5),
        az_s=dma(2, 2, 2),
        az_r=dma(2, 4),
        vz_s=dma(2, 2),
        vz_r=dma(4),
        last_sem=dma(3),
    )
    names = tuple(inputs) + tuple(outputs) + tuple(scratch)
    middle = pl.pallas_call(
        functools.partial(main_kernel, names, dp_count, head_count),
        out_shape=tuple(v[0] for v in outputs.values()),
        in_specs=[v[1] for v in inputs.values()],
        out_specs=tuple(v[1] for v in outputs.values()),
        scratch_shapes=list(scratch.values()),
        compiler_params=pltpu.CompilerParams(
            collective_id=0, has_side_effects=True, vmem_limit_bytes=VMEM_LIMIT
        ),
        name="layer",
    )(*(v[0] for v in inputs.values()))

    slice_b = HD // dp_count
    out = pl.pallas_call(
        functools.partial(end_kernel, mem_rows, hid, lanes),
        out_shape=(
            sds(2, 2, block, width),
            sds(2, text_rows, 2, width),
            sds(mem_rows, lanes, dtype=F32),
            sds(3, share, local, dtype=F32),
            sds(local // HD, 2, slice_b, dtype=F32),
            sds(local, share, dtype=F32),
            sds(hid, width, dtype=F32),
            sds(hid, width, dtype=F32),
            sds(1, hid, dtype=F32),
            sds(2, lanes, dtype=F32),
            sds(4, lanes, dtype=F32),
        ),
        in_specs=[INV] * 6,
        out_specs=tuple([INV] * 11),
        name="results",
    )(*middle)
    acts, d_text, d_init, d_qkv, d_bqv, d_wout, d_win, d_wback, d_bin, d_gains, d_biases = out
    return (
        acts, d_text.transpose(0, 2, 1, 3), d_init,
        d_qkv.transpose(1, 0, 2),
        d_bqv.transpose(1, 0, 2),
        d_wout, d_win.T, d_wback, d_bin[0], d_gains, d_biases,
    )


def solution(mesh):
    body = by_chip if mesh.shape["dp"] == 8 and mesh.shape["head"] == 4 else local
    return jax.shard_map(
        body,
        mesh=mesh,
        in_specs=(
            P("dp", None, "head", None),
            P("dp", None, None),
            P("dp", None),
            P("dp", None, None),
            P(None, ("dp", "head")),
            P(None, None, "head"),
            P(None, "head", None),
            P("head", None),
            P(None, ("dp", "head")),
            P(("dp", "head"), None),
            P(("dp", "head")),
            P(None, ("dp", "head")),
            P(None, ("dp", "head")),
            P("dp", None, "head", None),
        ),
        out_specs=(
            P("dp", None, "head", None),
            P("dp", None, "head", None),
            P(None, ("dp", "head")),
            P("dp", None, "head"),
            P(None, "head", "dp"),
            P("head", "dp"),
            P(None, ("dp", "head")),
            P(("dp", "head"), None),
            P(("dp", "head")),
            P(None, ("dp", "head")),
            P(None, ("dp", "head")),
        ),
        check_vma=False,
    )
```

profile of v0, /device:TPU:0, one launch (start us, length us, event | category | flops | bytes accessed | tf_op | source)
XLA Modules:
  0.0 173.1 jit_solution(14855309359430152513)
XLA Ops:
  0.6 169.1 %layer.1 = (bf16[2,2,128,768]{3,2,1,0:T(8,128)(2,1)}, bf16[2,123,2,768]{3,2,1,0:T(2,128)(2,1)}, f32[96,768]{1,0:T(8,128)}, f32[96,768]{1,0:T(8,128)}, f32[96,768]{1,0:T(8,128)}, /*index=5*/f32[16,128]{1,0:T(8,128)}) custom-call(bf16[2,123,2,768]{3,2,1,0:T(2,128)(2,1)} %bitcast.14, s32[2,2,492]{2,1,0:T(2,128)} %values_1_.1, s32[2,2]{1,0:T(2,128)} %values_2_.1, ...), custom_call_target="tpu_custom_call" | custom-call | tf_op jit(solution)/shard_map/layer/pallas_call | solution.py:1787
  169.7 3.3 %results.1 = (bf16[2,2,128,768]{3,2,1,0:T(8,128)(2,1)}, bf16[2,123,2,768]{3,2,1,0:T(2,128)(2,1)}, f32[10,24]{1,0:T(8,128)}, f32[3,96,192]{2,1,0:T(8,128)}, f32[3...) custom-call(bf16[2,2,128,768]{3,2,1,0:T(8,128)(2,1)} %get-tuple-elem, ...), custom_call_target="tpu_custom_call" | custom-call | tf_op jit(solution)/shard_map/results/pallas_call | solution.py:1800
where the time goes:
time: 173 us
  Pallas kernels  172 us (99%)
    pallas_call x1, Pallas kernels, by_chip(): pl.pallas_call(functools.partial(main_kernel, names, dp_count, head_count...  169 us

commit v1 on v0

--- a/solution.py
+++ b/solution.py
@@ -474,6 +474,14 @@
 
     column_size = 2 * head_count - 1
 
+    def sent_rows(count, sem):
+        ref = wf.at[0, pl.ds(0, count)]
+        push(ref, ref, sem, sem, sibling).wait_send()
+
+    def got_rows(count, sem):
+        ref = wf.at[0, pl.ds(0, count)]
+        push(ref, ref, sem, sem, sibling).wait_recv()
+
     def when_not(cond, body):
         pl.when(jnp.logical_not(cond))(body)
 
@@ -530,7 +538,7 @@
 
     def rows_out(a, j, h):
         return push(
-            rows_src(a, j, h), rows_dst(a, z, h), r_.rows_s.at[a, j, h], r_.rows_r.at[a, z],
+            rows_src(a, j, h), rows_dst(a, z, h), r_.rows_s.at[a], r_.rows_r.at[a, z],
             device(h, px, py, 2 * core + j),
         )
 
@@ -546,7 +554,7 @@
 
     def rows_forward(a, zs, h):
         ref = rows_dst(a, zs, h)
-        return push(ref, ref, r_.fwd_s.at[a, zs], r_.fwd_r.at[a, zs], sibling)
+        return push(ref, ref, r_.fwd_s.at[a], r_.fwd_r.at[a], sibling)
 
     def rows_pass(a):
         for zs in range(head_count):
@@ -555,21 +563,18 @@
             when_not(
                 here,
                 lambda: push(
-                    rows_src(a, 0, 0), rows_dst(a, zs, core), r_.rows_s.at[a, 0, 0], r_.rows_r.at[a, zs], sibling
+                    rows_src(a, 0, 0), rows_dst(a, zs, core), r_.rows_s.at[a], r_.rows_r.at[a, zs], sibling
                 ).wait_recv(),
             )
             rows_forward(a, zs, core).start()
 
     def rows_ready(a):
-        for zs in range(head_count):
-            rows_forward(a, zs, 1 - core).wait_recv()
+        got_rows(head_count * piece, r_.fwd_r.at[a])
 
     def rows_done(a):
-        for j in range(2):
-            for h in range(2):
-                when_not((core == h) & (z == 2 * core + j), lambda: rows_out(a, j, h).wait_send())
-        for zs in range(head_count):
-            rows_forward(a, zs, core).wait_send()
+        pl.when(is_home)(lambda: sent_rows(3 * piece, r_.rows_s.at[a]))
+        pl.when(away)(lambda: sent_rows(4 * piece, r_.rows_s.at[a]))
+        sent_rows(head_count * piece, r_.fwd_s.at[a])
 
     def hidden_block(p, zi):
         return pl.ds(pl.multiple_of((zi * planes + p) * hid, hid), hid)
@@ -608,7 +613,7 @@
             (x_plane, y_mate) if kind == 0 else (y_plane, x_mate),
         )[which]
         ref = wf.at[kind, hidden_block(p, zi)]
-        return push(ref, ref, r_.side_s.at[zi, kind, which], r_.side_r.at[zi, kind, which], mate)
+        return push(ref, ref, r_.side_s.at[0], r_.side_r.at[zi, kind, which], mate)
 
     def side_first(zi):
         for kind in range(2):
@@ -630,11 +635,10 @@
         side(1, zi, 2).wait_recv()
 
     def small_out(i):
-        return push(r_.small, r_.small_all.at[me], r_.small_s.at[i], r_.small_r.at[z, core], column(i)[1])
-
-    def small_in(i):
-        at, (dp_i, z_i) = column(i)
-        return push(r_.small, r_.small_all.at[at], r_.small_s.at[i], r_.small_r.at[z_i, dp_i % 2], sibling)
+        return push(r_.small, r_.small_all.at[me], r_.small_s.at[0], r_.small_r.at[0], column(i)[1])
+
+    every_small = r_.small_all.at[pl.ds(0, column_size)]
+    smalls = push(every_small, every_small, r_.small_s.at[0], r_.small_r.at[0], sibling)
 
     def small_plane(i):
         p, mate = ((plane, x_mate), (plane, y_mate), (x_plane, y_mate))[i]
@@ -650,8 +654,13 @@
     mates = [x_mate, y_mate] + [column(i)[1] for i in range(column_size)]
     for mate in mates:
         pl.semaphore_signal(barrier, inc=1, device_id=mate, device_id_type=MESH)
-    wf[0, hidden_block(plane, z), :] = r_.w_in_t[...]
-    wf[1, hidden_block(plane, z), :] = r_.w_back[...]
+    early = [
+        pltpu.make_async_copy(r_.w_in_t, wf.at[0, hidden_block(plane, z)], r_.early_sem.at[0]),
+        pltpu.make_async_copy(r_.w_back, wf.at[1, hidden_block(plane, z)], r_.early_sem.at[1]),
+        pltpu.make_async_copy(r_.text, r_.text_v, r_.early_sem.at[2]),
+    ]
+    for copy in early:
+        copy.start()
     vtmp = r_.vtmp
     vtmp[...] = jnp.zeros_like(vtmp)
     vtmp[0:2, 0:lanes] = r_.norm_gains[...].astype(F32)
@@ -668,6 +677,8 @@
 
     for i in range(column_size):
         small_out(i).start()
+    early[0].wait()
+    early[1].wait()
     side_first(z)
     ffn_own()
     attention_outs(lambda c: c.start())
@@ -695,11 +706,12 @@
         copy.start()
 
     def pad_text(j):
-        both = r_.text[j].astype(F32)
+        both = r_.text_v[j].astype(F32)
         for s in range(2):
             r_.text_pad[j, s, 0:text_rows, :] = both[:, s, :].astype(BF)
             r_.text_pad[j, s, text_rows:step, :] = jnp.zeros((step - text_rows, width), BF)
 
+    early[2].wait()
     loop(2, pad_text)
     for ref in (r_.sg, r_.dinit, r_.dbin, r_.carry, r_.rs):
         ref[...] = jnp.zeros_like(ref)
@@ -716,8 +728,7 @@
         attention_plane(k, 1).wait_recv()
         attention_plane(k, 3).start()
 
-    for i in range(column_size):
-        small_in(i).wait_recv()
+    smalls.wait_recv()
     small_plane(0).start()
     small_plane(1).start()
     ffn_two(0)
@@ -803,6 +814,13 @@
     def taken(slot, at):
         return acc[at, :] + r_.recv_buf[slot, at, :].astype(F32)
 
+    def by_quarter(slot, body):
+        def one(r):
+            exchange(slot, (rows(r), r)).wait()
+            body(rows(r))
+
+        loop(head_count, one)
+
     def by_half(slot, body):
         def one(r):
             pl.when(r % 2 == 0)(lambda: exchange(slot, half_span(r // 2)).wait())
@@ -829,7 +847,7 @@
         zt = (z + i) % head_count
         src, dst = back_copy(which, seg, zt)
         return push(
-            src, dst, r_.back_s.at[which, seg, i], r_.back_r.at[which, seg, z % 2, core], device(z // 2, px, py, zt)
+            src, dst, r_.back_s.at[which, seg], r_.back_r.at[which, seg], device(z // 2, px, py, zt)
         )
 
     def back_here(which, seg):
@@ -843,33 +861,28 @@
             back_out(which, seg, i).start()
 
     def back_sent(which, seg):
-        pl.when(is_home)(lambda: back_here(which, seg).wait())
-        pl.when(away)(lambda: back_out(which, seg, 0).wait_send())
-        for i in range(1, head_count):
-            back_out(which, seg, i).wait_send()
-
-    def back_done(which, seg):
-        dst = (r_.acts_o, r_.text_pad)[which]
-        for j in range(2):
-            for h in range(2):
-                when_not(
-                    (core == h) & (z == 2 * core + j),
-                    lambda: push(
-                        r_.text_all.at[seg, pl.ds(0, piece)], dst.at[j, seg, pl.ds(h * piece, piece)],
-                        r_.back_s.at[which, seg, 0], r_.back_r.at[which, seg, j, h], sibling,
-                    ).wait_recv(),
-                )
+        def home():
+            back_here(which, seg).wait()
+            sent_rows(3 * piece, r_.back_s.at[which, seg])
+            got_rows(3 * piece, r_.back_r.at[which, seg])
+
+        def not_home():
+            sent_rows(4 * piece, r_.back_s.at[which, seg])
+            got_rows(4 * piece, r_.back_r.at[which, seg])
+
+        pl.when(is_home)(home)
+        pl.when(away)(not_home)
 
     def tail_z(which, i):
         zt = (z + 1 + i) % head_count
         to = device(core, px, py, zt)
         dst = r_.factors.at[which, z, plane]
-        return push(r_.factor_out.at[which, zt], dst, r_.tg_s.at[which, i], r_.tg_r.at[which, z], to)
+        return push(r_.factor_out.at[which, zt], dst, r_.tg_s.at[which], r_.tg_r.at[which, z], to)
 
     def tail_z_in(which, i):
         zs = (z + 1 + i) % head_count
         dst = r_.factors.at[which, zs, plane]
-        return push(r_.factor_out.at[which, zs], dst, r_.tg_s.at[which, i], r_.tg_r.at[which, zs], sibling)
+        return push(r_.factor_out.at[which, zs], dst, r_.tg_s.at[which], r_.tg_r.at[which, zs], sibling)
 
     def tail_plane(which, i):
         p, zs, to = (
@@ -877,7 +890,7 @@
             (x_plane, pl.ds(0, 2), y_mate), (y_plane, pl.ds(2, 2), x_mate),
         )[i]
         buf = r_.factors.at[which, zs, p]
-        return push(buf, buf, r_.tg_s.at[which, 3 + i], r_.tg_r.at[which, head_count + i], to)
+        return push(buf, buf, r_.tg_s.at[which], r_.tg_r.at[which, head_count + i], to)
 
     def tail_pair(which):
         src = r_.factors.at[which, :, :, :, pl.ds(0, half_width)]
@@ -902,10 +915,7 @@
                 tail_plane(which, 2 + i).wait_recv()
             tail_pair(which).start()
         else:
-            for i in range(head_count - 1):
-                tail_z(which, i).wait_send()
-            for i in range(4):
-                tail_plane(which, i).wait_send()
+            sent_rows((head_count - 1 + 3 * head_count) * tail, r_.tg_s.at[which])
 
     half_width = width // 2
 
@@ -982,17 +992,17 @@
             pt[seg, h] = p
             ot[seg, j, head_rows(h, 0), :] = nn(v, p).astype(BF)
 
-        loop(heads, one, unroll=2)
+        loop(heads, one, unroll=3)
 
     def out_project(seg):
         def one(i):
-            span = half_span(i)
+            span = (rows(i), i)
             at = span[0]
             give(
                 0, span, tn(ot[seg, 0, :, at], wa[0, 3 * local :, :]) + tn(ot[seg, 1, :, at], wa[1, 3 * local :, :])
             )
 
-        loop(2, one)
+        loop(head_count, one)
 
     def norm_one(seg):
         def one(at):
@@ -1003,7 +1013,7 @@
             hf[at, :] = h
             r_.hb[seg, at, :] = h.astype(BF)
 
-        by_half(0, one)
+        by_quarter(0, one)
 
     def inner(seg, at):
         v = nt(r_.hb[seg], wf[0, at, :]) + r_.bin_row[:, at]
@@ -1018,10 +1028,10 @@
 
     def outer(seg):
         def one(i):
-            span = half_span(i)
+            span = (rows(i), i)
             give(1, span, nn(r_.u[seg, span[0], :], wf[1]))
 
-        loop(2, one)
+        loop(head_count, one)
 
     def norm_two(seg):
         def one(at):
@@ -1030,13 +1040,36 @@
             keep_scale(1, seg, at, scale)
             r_.y[seg, at, :] = (hat * par[1:2, :] + par[5:6, :]).astype(BF)
 
-        by_half(1, one)
+        by_quarter(1, one)
 
     def next_memory():
         last = r_.y[0, tail_at, :].astype(F32)
         memory = jnp.where(is_mem, jnp.where(flags[1] > 0, par[...], last), 0.0)
         r_.cur_b[...] = memory.astype(BF)
         r_.cur_a[...] = pltpu.roll(memory, mem_rows, 0).astype(BF)
+
+    def pull_two_part(g_y, hat, scale):
+        pre = pull_norm(g_y * par[1:2, :], hat, scale)
+        r_.sg[1:2, :] += row_sum(g_y * hat)
+        r_.sg[5:6, :] += row_sum(g_y)
+        r_.sg[4:5, :] += row_sum(pre)
+        return pre.astype(BF)
+
+    def pull_two():
+        def one(n):
+            seg, r = 1 - n // head_count, n % head_count
+            pl.when(n == head_count)(lambda: rows_ready(2))
+            below = lax.broadcasted_iota(jnp.int32, (step, width), 0) + r * step
+            held = (below >= seg_len - tail) & (seg == 0)
+            g_y = jnp.where(held, 0.0, r_.cot_all[seg, rows(r), :].astype(F32))
+            hat = r_.xh2[seg, rows(r), :].astype(F32)
+            r_.xh2[seg, rows(r), :] = pull_two_part(g_y, hat, kept_scale(1, seg, rows(r)))
+
+        loop(2 * head_count, one)
+
+    def keep_tail():
+        r_.xh2_t[...] = r_.xh2[0, tail_at, :]
+        r_.gp_t[...] = r_.gp[0, tail_at, :]
 
     pl.when(inside)(lambda: ffn_hop_on(3))
     pl.when(depth == 0)(lambda: ffn_hop_on(2))
@@ -1121,29 +1154,6 @@
     loop(2, forward)
     back_send(0, 1)
     rows_ready(3)
-
-    def pull_two_part(g_y, hat, scale):
-        pre = pull_norm(g_y * par[1:2, :], hat, scale)
-        r_.sg[1:2, :] += row_sum(g_y * hat)
-        r_.sg[5:6, :] += row_sum(g_y)
-        r_.sg[4:5, :] += row_sum(pre)
-        return pre.astype(BF)
-
-    def pull_two():
-        def one(n):
-            seg, r = 1 - n // head_count, n % head_count
-            pl.when(n == head_count)(lambda: rows_ready(2))
-            below = lax.broadcasted_iota(jnp.int32, (step, width), 0) + r * step
-            held = (below >= seg_len - tail) & (seg == 0)
-            g_y = jnp.where(held, 0.0, r_.cot_all[seg, rows(r), :].astype(F32))
-            hat = r_.xh2[seg, rows(r), :].astype(F32)
-            r_.xh2[seg, rows(r), :] = pull_two_part(g_y, hat, kept_scale(1, seg, rows(r)))
-
-        loop(2 * head_count, one)
-
-    def keep_tail():
-        r_.xh2_t[...] = r_.xh2[0, tail_at, :]
-        r_.gp_t[...] = r_.gp[0, tail_at, :]
 
     def pull_tail():
         g_y = r_.cot_all[0, tail_at, :].astype(F32) + r_.carry[...]
@@ -1201,7 +1211,7 @@
             for part, value in enumerate((d_q, d_k, d_v)):
                 qkv[seg, j, head_rows(h, part), :] = value
 
-        loop(heads, one, unroll=2)
+        loop(heads, one, unroll=3)
 
     def pull_rows(seg, span):
         at = span[0]
@@ -1241,11 +1251,11 @@
 
     def sum_one(name, kind, b):
         buf, got, s, r = parts_of(name)(kind)
-        return push(cut(buf, kind, 1, b), got[0].at[b], s.at[b], r.at[b], sum_mates[kind][0])
+        return push(cut(buf, kind, 1, b), got[0].at[b], s, r.at[b], sum_mates[kind][0])
 
     def sum_two(name, kind):
         buf, got, s, r = parts_of(name)(kind)
-        return push(cut(buf, kind, 0, 1), got[1], s.at[2], r.at[2], sum_mates[kind][1])
+        return push(cut(buf, kind, 0, 1), got[1], s, r.at[2], sum_mates[kind][1])
 
     def ffn_sum(d):
         zi = order_at(d)
@@ -1253,7 +1263,7 @@
         def parts(kind):
             return (
                 r_.fsend.at[kind, zi], (r_.f_one.at[kind, zi], r_.f_two.at[kind, zi]),
-                r_.fsum_s.at[kind, zi], r_.fsum_r.at[kind, zi],
+                r_.sum_s.at[0], r_.fsum_r.at[kind, zi],
             )
 
         return parts
@@ -1264,24 +1274,24 @@
         def parts(kind):
             return (
                 r_.asend.at[n, kind], (r_.a_one.at[n, kind], r_.a_two.at[n, kind]),
-                r_.asum_s.at[n, kind], r_.asum_r.at[n, kind],
+                r_.sum_s.at[1], r_.asum_r.at[n, kind],
             )
 
         return parts
 
-    halves = ("a", "b")
+    halves = ("a", "b", "c")
     for n, name in enumerate(halves):
         sums[name] = attention_sum(n)
     sums["v"] = lambda kind: (
-        r_.vsend.at[kind], (r_.v_one.at[kind], r_.v_two.at[kind]), r_.vsum_s.at[kind], r_.vsum_r.at[kind]
+        r_.vsend.at[kind], (r_.v_one.at[kind], r_.v_two.at[kind]), r_.sum_s.at[2], r_.vsum_r.at[kind]
     )
 
     def start_sum(name, which=((1, 0), (1, 1), (0, 0), (0, 1))):
         for b, kind in which:
             sum_one(name, kind, b).start()
 
-    def travel(name):
-        for kind in range(2):
+    def travel(name, kinds=(0, 1)):
+        for kind in kinds:
             buf, got, _, _ = parts_of(name)(kind)
             sum_one(name, kind, 1).wait_recv()
             add_all(cut(buf, kind, 0, 1), got[0].at[1])
@@ -1294,11 +1304,12 @@
             sum_two(name, kind).wait_recv()
             add_all(cut(buf, kind, 0, 0), got[0].at[0], got[1])
 
-    def sum_sent(name):
-        for kind in range(2):
-            for b in range(2):
-                sum_one(name, kind, b).wait_send()
-            sum_two(name, kind).wait_send()
+    def sums_sent():
+        every = r_.fsend.at[:, pl.ds(0, 3)]
+        push(every, every, r_.sum_s.at[0], r_.sum_s.at[0], sibling).wait_send()
+        sent_rows(12 * hid_rows, r_.sum_s.at[1])
+        every = r_.small_all.at[pl.ds(0, 12)]
+        push(every, every, r_.sum_s.at[2], r_.sum_s.at[2], sibling).wait_send()
 
     def z_out(kind, d):
         slot = jnp.where(inside, jnp.where(d == 1, 0, jnp.where(d == 2, 4, 1)), jnp.where(d == 1, 0, d))
@@ -1341,11 +1352,12 @@
 
     def last_here(name, k):
         buf, dst, _, _ = last[name]
-        return pltpu.make_async_copy(cut(buf.at[k], k, 0, 0).at[core], dst.at[z], r_.last_sem.at["abv".index(name)])
+        return pltpu.make_async_copy(cut(buf.at[k], k, 0, 0).at[core], dst.at[z], r_.last_sem.at["abcv".index(name)])
 
     last = {
         "a": (r_.asend.at[0], r_.a_z.at[0], r_.az_s.at[0], r_.az_r.at[0]),
         "b": (r_.asend.at[1], r_.a_z.at[1], r_.az_s.at[1], r_.az_r.at[1]),
+        "c": (r_.asend.at[2], r_.a_z.at[2], r_.az_s.at[2], r_.az_r.at[2]),
         "v": (r_.vsend, r_.v_z, r_.vz_s, r_.vz_r),
     }
 
@@ -1379,19 +1391,16 @@
                 r_.fsend[kind, i, p // 2, p % 2] = value[p * hid : (p + 1) * hid, :].astype(BF)
 
         grads(1, r_.u, r_.xh2)
-
-        def first_kind():
-            pl.when(d == 2)(lambda: travel(3))
-            start_sum(d, ((1, 1), (0, 1)))
-
-        pl.when(d >= 2)(first_kind)
+        pl.when(d >= 2)(lambda: start_sum(d, ((1, 1), (0, 1))))
         pull_inner(i)
         grads(0, r_.gp, r_.hb)
+        pl.when(d == 2)(lambda: travel(3, (1,)))
         pl.when(d >= 2)(lambda: start_sum(d, ((1, 0), (0, 0))))
+        pl.when(d == 1)(lambda: travel(3, (0,)))
 
     keep_tail()
+    tail_gather(0, 1)
     pull_two()
-    tail_gather(0, 1)
     loop(head_count, lambda n: ffn_grads(head_count - 1 - n))
     dbin_pair = push(r_.dbin, r_.dbin_in, r_.pair_s.at[2], r_.pair_r.at[2], sibling)
 
@@ -1402,7 +1411,6 @@
         pull_one(seg)
 
         def first_events():
-            end_ffn(3)
             travel(2)
             start_sum(1)
             start_sum(0)
@@ -1412,6 +1420,7 @@
         pull_heads(seg)
 
         def segment_two():
+            end_ffn(3)
             loop(2, lambda i: pull_rows(1, end_span(i)))
 
             def one(i):
@@ -1437,7 +1446,7 @@
     travel(0)
     z_pass(2)
     hid_rows = width // dp_count
-    cut_rows = hid_rows // 2
+    cut_rows = hid_rows // len(halves)
 
     def attention_grads(i):
         wide = width // 2
@@ -1447,10 +1456,11 @@
         for k in range(2):
             qkv_g = nt(xt[0], qkv[0, k]) + nt(xt[1], qkv[1, k])
             out_g = nt(gt[0], ot[0, k]) + nt(gt[1], ot[1, k])
-            for b in range(8):
-                at = slice(b * cut_rows, (b + 1) * cut_rows)
-                r_.asend[b % 2, k, i, b // 4, (b // 2) % 2, :, 0 : 3 * local] = qkv_g[at, :].astype(BF)
-                r_.asend[b % 2, k, i, b // 4, (b // 2) % 2, :, 3 * local :] = out_g[at, :].astype(BF)
+            for n in range(4 * len(halves)):
+                at = slice(n * cut_rows, (n + 1) * cut_rows)
+                b, part = n // len(halves), n % len(halves)
+                r_.asend[part, k, i, b // 2, b % 2, :, 0 : 3 * local] = qkv_g[at, :].astype(BF)
+                r_.asend[part, k, i, b // 2, b % 2, :, 3 * local :] = out_g[at, :].astype(BF)
 
     def both_planes(n):
         attention_grads(jnp.where(n == 0, 1 - py, py))
@@ -1529,19 +1539,32 @@
     text_grad(0)
     back_send(1, 0)
     travel("b")
+    start_sum("c", ((0, 1), (0, 0)))
+    travel("c")
     travel("v")
     end_plane("a")
     last_each("a", lambda c: c.start(), lambda c: c.start())
     tail_gather(1, 2)
+    end_plane("b")
+    last_each("b", lambda c: c.start(), lambda c: c.start())
     end_plane("v")
     last_each("v", lambda c: c.start(), lambda c: c.start())
-    end_plane("b")
-    last_each("b", lambda c: c.start(), lambda c: c.start())
+    end_plane("c")
+    last_each("c", lambda c: c.start(), lambda c: c.start())
+
+    results = (
+        (r_.win_v, r_.win_o), (r_.wback_v, r_.wback_o), (r_.dt_v, r_.dt_o), (r_.dqkv_v, r_.dqkv_o),
+        (r_.dwout_v, r_.dwout_o), (r_.dinit_v, r_.dinit_o), (r_.dbqv_v, r_.dbqv_o), (r_.dbin_v, r_.dbin_o),
+        (r_.dgains_v, r_.dgains_o), (r_.dbiases_v, r_.dbiases_o),
+    )
+
+    def leave(n):
+        return pltpu.make_async_copy(results[n][0], results[n][1], r_.leave_sem.at[n])
 
     tail_gather(0, 3)
     tail_gather(1, 3)
     extra = tail_products()
-    for kind, out in enumerate((r_.win_o, r_.wback_o)):
+    for kind, out in enumerate((r_.win_v, r_.wback_v)):
         value = cut(r_.fsend.at[kind, z], kind, 0, 0)[...].astype(F32)
         z_in(kind, 0).wait_recv()
         out[...] = value + r_.f_z[kind, 0].astype(F32)
@@ -1553,17 +1576,16 @@
         pl.when(inside)(other_side)
         out[:, half_of(core)] += extra[kind][0]
         out[:, half_of(1 - core)] += extra[kind][1]
-
-
-    for name in (0, 1, 2, 3, "a", "b", "v"):
-        sum_sent(name)
+        leave(kind).start()
+
+
+    sums_sent()
     for d in range(1, head_count):
         for kind in range(2):
             z_out(kind, d).wait_send()
     for which in range(2):
         for seg in range(2):
             back_sent(which, seg)
-            back_done(which, seg)
     for a in range(2, 4):
         rows_done(a)
     attention_outs(lambda c: c.wait_send())
@@ -1579,21 +1601,38 @@
                 attention_plane(k, which).wait_send()
 
         pl.when(foreign[k])(sent)
-    for zi in range(head_count):
-        for kind in range(2):
-            for which in range(3):
-                side(kind, zi, which).wait_send()
-    for i in range(column_size):
-        small_out(i).wait_send()
+    every_side = wf.at[:, pl.ds(0, 3 * head_count * hid)]
+    push(every_side, every_side, r_.side_s.at[0], r_.side_s.at[0], sibling).wait_send()
+    smalls.wait_send()
     for i in range(3):
         small_plane(i).wait_send()
     for j in range(2):
         both = [r_.text_pad[j, s, 0:text_rows, :].astype(F32)[:, None, :] for s in range(2)]
-        r_.dt_o[j] = jnp.concatenate(both, axis=1).astype(BF)
-    r_.att_o[0:cut_rows, :] = last_total("a")
-    r_.att_o[cut_rows:hid_rows, :] = last_total("b")
-    r_.vec_o[...] = last_total("v")
-    for name in "abv":
+        r_.dt_v[j] = jnp.concatenate(both, axis=1).astype(BF)
+    leave(2).start()
+    total_v = last_total("v")
+    r_.dinit_v[...] = total_v[6 : 6 + mem_rows, 0:lanes]
+    for b in range(per_block):
+        for part in range(2):
+            at = 32 + (part * per_block + b) * piece_b
+            r_.dbqv_v[b, part : part + 1, :] = total_v[1:2, at : at + piece_b]
+    r_.dbin_v[...] = total_v[0:1, 32 : 32 + hid]
+    r_.dgains_v[...] = total_v[0:2, 0:lanes]
+    r_.dbiases_v[...] = total_v[2:6, 0:lanes]
+    for n in range(5, len(results)):
+        leave(n).start()
+    for n, name in enumerate(halves):
+        part = last_total(name)
+        at = slice(n * cut_rows, (n + 1) * cut_rows)
+        for t in range(3):
+            r_.dqkv_v[t, at, :] = part[:, t * local : (t + 1) * local]
+        r_.out_rows[at, :] = part[:, 3 * local :]
+    leave(3).start()
+    r_.dwout_v[...] = r_.out_rows[...].T
+    leave(4).start()
+    for n in range(len(results)):
+        leave(n).wait()
+    for name in "abcv":
         last_each(name, None, lambda c: c.wait_send())
 
 
@@ -1618,25 +1657,32 @@
 INS = pl.BlockSpec(memory_space=pltpu.SMEM)
 
 
-def end_kernel(mem_rows, hid, lanes, acts, dt, win, wback, att, vec, *outs):
-    acts_o, dt_o, dinit_o, dqkv_o, dbqv_o, dwout_o, dwin_o, dwback_o, dbin_o, dgains_o, dbiases_o = outs
-    acts_o[...] = acts[...]
-    dt_o[...] = dt[...]
-    dinit_o[...] = vec[6 : 6 + mem_rows, 0:lanes]
-    parts, _, local_width = dqkv_o.shape
-    for t in range(parts):
-        dqkv_o[t] = att[:, t * local_width : (t + 1) * local_width]
-    per_block, _, slice_b = dbqv_o.shape
-    for b in range(per_block):
-        for part in range(2):
-            at = 32 + (part * per_block + b) * slice_b
-            dbqv_o[b, part : part + 1, :] = vec[1:2, at : at + slice_b]
-    dwout_o[...] = att[:, parts * local_width :].T
-    dwin_o[...] = win[...]
-    dwback_o[...] = wback[...]
-    dbin_o[...] = vec[0:1, 32 : 32 + hid]
-    dgains_o[...] = vec[0:2, 0:lanes]
-    dbiases_o[...] = vec[2:6, 0:lanes]
+def end_kernel(count, *refs):
+    given, out, kept = refs[:count], refs[count : 2 * count], refs[2 * count : 3 * count]
+    sem = refs[3 * count]
+    parts = []
+    for n in range(count):
+        if len(given[n].shape) == 4:
+            parts += [(n, (j, s)) for j in range(2) for s in range(2)] if n == 0 else [(n, (j,)) for j in range(2)]
+        else:
+            parts.append((n, ()))
+
+    def part(ref, at):
+        return ref.at[at] if at else ref
+
+    loads = [
+        pltpu.make_async_copy(part(given[n], at), part(kept[n], at), sem.at[0, i]) for i, (n, at) in enumerate(parts)
+    ]
+    stores = [
+        pltpu.make_async_copy(part(kept[n], at), part(out[n], at), sem.at[1, i]) for i, (n, at) in enumerate(parts)
+    ]
+    for copy in loads:
+        copy.start()
+    for load, store in zip(loads, stores):
+        load.wait()
+        store.start()
+    for copy in stores:
+        copy.wait()
 
 
 def by_chip(
@@ -1659,7 +1705,7 @@
     share = width // dp_count
 
     inputs = dict(
-        text=(text.transpose(0, 2, 1, 3), INV),
+        text=(text.transpose(0, 2, 1, 3), ANY),
         boundary=(boundary, INV),
         reset=(reset, INS),
         memory_in=(memory_in.transpose(1, 0, 2), INV),
@@ -1667,23 +1713,33 @@
         wq_t=(w_qkv.transpose(1, 2, 0).reshape(3 * local, width), ANY),
         w_out=(w_out, ANY),
         b_qv=(b_qv.transpose(1, 0, 2), INV),
-        w_in_t=(w_in.T, INV),
-        w_back=(w_back, INV),
+        w_in_t=(w_in.T, ANY),
+        w_back=(w_back, ANY),
         b_in=(b_in[None, :], INV),
         norm_gains=(norm_gains, INV),
         biases=(biases, INV),
         cotangent=(cotangent, ANY),
     )
-    outputs = dict(
-        acts_o=(sds(2, 2, block, width), ANY),
-        dt_o=(sds(2, text_rows, 2, width), INV),
-        win_o=(sds(hid, width, dtype=F32), INV),
-        wback_o=(sds(hid, width, dtype=F32), INV),
-        att_o=(sds(share, width, dtype=F32), INV),
-        vec_o=(sds(16, 128, dtype=F32), INV),
+    slice_b = HD // dp_count
+    shapes = dict(
+        acts=sds(2, 2, block, width),
+        dt=sds(2, text_rows, 2, width),
+        dinit=sds(mem_rows, lanes, dtype=F32),
+        dqkv=sds(3, share, local, dtype=F32),
+        dbqv=sds(local // HD, 2, slice_b, dtype=F32),
+        dwout=sds(local, share, dtype=F32),
+        win=sds(hid, width, dtype=F32),
+        wback=sds(hid, width, dtype=F32),
+        dbin=sds(1, hid, dtype=F32),
+        dgains=sds(2, lanes, dtype=F32),
+        dbiases=sds(4, lanes, dtype=F32),
     )
+    outputs = {name + "_o": (shape, ANY) for name, shape in shapes.items()}
+    staged = {name + "_v": pltpu.VMEM(shape.shape, shape.dtype) for name, shape in shapes.items() if name != "acts"}
     scratch = dict(
         text_pad=vmem(2, 2, block, width),
+        text_v=vmem(2, text_rows, 2, width),
+        early_sem=dma(3),
         text_all=vmem(2, seg_len, width),
         cot_all=vmem(2, seg_len, width),
         wa=vmem(2, 4 * local, width),
@@ -1732,16 +1788,17 @@
         f_one=vmem(2, head_count, 2, hid, width),
         f_two=vmem(2, head_count, hid, width),
         f_z=vmem(2, head_count + 1, hid, width),
-        asend=vmem(2, 2, 2, 2, 2, share // 2, width),
-        a_one=vmem(2, 2, 2, 2, share // 2, width),
-        a_two=vmem(2, 2, 2, share // 2, width),
-        a_z=vmem(2, head_count, share // 2, width),
+        asend=vmem(3, 2, 2, 2, 2, share // 3, width),
+        a_one=vmem(3, 2, 2, 2, share // 3, width),
+        a_two=vmem(3, 2, 2, share // 3, width),
+        a_z=vmem(3, head_count, share // 3, width),
+        out_rows=f32(share, local),
         vsend=vmem(2, 2, 2, 2, 16, 128),
         v_one=vmem(2, 2, 2, 16, 128),
         v_two=vmem(2, 2, 16, 128),
         v_z=vmem(head_count, 16, 128),
-        small_s=dma(7),
-        small_r=dma(4, 2),
+        small_s=dma(1),
+        small_r=dma(1),
         small_ps=dma(3),
         small_pr=dma(3),
         pair_s=dma(3),
@@ -1751,38 +1808,38 @@
         plane_s=dma(2, 4),
         plane_r=dma(2, 4),
         local_sem=dma(2),
-        rows_s=dma(4, 2, 2),
+        rows_s=dma(4),
         rows_r=dma(4, 4),
         here_sem=dma(4),
-        fwd_s=dma(4, 4),
-        fwd_r=dma(4, 4),
+        fwd_s=dma(4),
+        fwd_r=dma(4),
         ffn_s=dma(5),
         ffn_r=dma(4),
-        side_s=dma(4, 2, 3),
+        side_s=dma(1),
         side_r=dma(4, 2, 3),
         send_sem=dma(2, 4),
         recv_sem=dma(2, 4),
-        back_s=dma(2, 2, 4),
-        back_r=dma(2, 2, 2, 2),
+        back_s=dma(2, 2),
+        back_r=dma(2, 2),
         back_here_sem=dma(2, 2),
-        fsum_s=dma(2, 4, 3),
+        sum_s=dma(3),
         fsum_r=dma(2, 4, 3),
-        asum_s=dma(2, 2, 3),
-        asum_r=dma(2, 2, 3),
-        tg_s=dma(2, 7),
+        asum_r=dma(3, 2, 3),
+        tg_s=dma(2),
         tg_r=dma(2, 8),
         tp_s=dma(2),
         tp_r=dma(2),
-        vsum_s=dma(2, 3),
         vsum_r=dma(2, 3),
         fz_s=dma(2, 4),
         fz_r=dma(2, 5),
-        az_s=dma(2, 2, 2),
-        az_r=dma(2, 4),
+        az_s=dma(3, 2, 2),
+        az_r=dma(3, 4),
+        leave_sem=dma(10),
         vz_s=dma(2, 2),
         vz_r=dma(4),
-        last_sem=dma(3),
+        last_sem=dma(4),
     )
+    scratch.update(staged)
     names = tuple(inputs) + tuple(outputs) + tuple(scratch)
     middle = pl.pallas_call(
         functools.partial(main_kernel, names, dp_count, head_count),
@@ -1796,24 +1853,12 @@
         name="layer",
     )(*(v[0] for v in inputs.values()))
 
-    slice_b = HD // dp_count
     out = pl.pallas_call(
-        functools.partial(end_kernel, mem_rows, hid, lanes),
-        out_shape=(
-            sds(2, 2, block, width),
-            sds(2, text_rows, 2, width),
-            sds(mem_rows, lanes, dtype=F32),
-            sds(3, share, local, dtype=F32),
-            sds(local // HD, 2, slice_b, dtype=F32),
-            sds(local, share, dtype=F32),
-            sds(hid, width, dtype=F32),
-            sds(hid, width, dtype=F32),
-            sds(1, hid, dtype=F32),
-            sds(2, lanes, dtype=F32),
-            sds(4, lanes, dtype=F32),
-        ),
-        in_specs=[INV] * 6,
-        out_specs=tuple([INV] * 11),
+        functools.partial(end_kernel, len(shapes)),
+        out_shape=tuple(shapes.values()),
+        in_specs=[ANY] * len(shapes),
+        out_specs=tuple([ANY] * len(shapes)),
+        scratch_shapes=[pltpu.VMEM(shape.shape, shape.dtype) for shape in shapes.values()] + [dma(2, 16)],
         name="results",
     )(*middle)
     acts, d_text, d_init, d_qkv, d_bqv, d_wout, d_win, d_wback, d_bin, d_gains, d_biases = out

time: 173 us -> 167 us (0.965)
  Pallas kernels: 172 us -> 166 us
    pallas_call x1, Pallas kernels: 169 us -> 163 us  [by_chip(): pl.pallas_call(functools.partial(main_kernel, names, dp_count, head_count...]
where the time goes in v1:
time: 167 us
  Pallas kernels  166 us (99%)
    pallas_call x1, Pallas kernels, by_chip(): pl.pallas_call(functools.partial(main_kernel, names, dp_count, head_count...  163 us

profile of v1, /device:TPU:0, one launch (start us, length us, event | category | flops | bytes accessed | tf_op | source)
XLA Modules:
  0.0 166.9 jit_solution(13840971456701061959)
XLA Ops:
  0.6 163.3 %layer.1 = (bf16[2,2,128,768]{3,2,1,0:T(8,128)(2,1)}, bf16[2,123,2,768]{3,2,1,0:T(2,128)(2,1)}, f32[10,24]{1,0:T(8,128)}, f32[3,96,192]{2,1,0:T(8,128)}, f32[3,2...) custom-call(bf16[2,123,2,768]{3,2,1,0:T(2,128)(2,1)} %bitcast.14, ...), custom_call_target="tpu_custom_call" | custom-call | tf_op jit(solution)/shard_map/layer/pallas_call | solution.py:1844
  163.9 2.8 %results.1 = (bf16[2,2,128,768]{3,2,1,0:T(8,128)(2,1)}, bf16[2,123,2,768]{3,2,1,0:T(2,128)(2,1)}, f32[10,24]{1,0:T(8,128)}, f32[3,96,192]{2,1,0:T(8,128)}, f32[3...) custom-call(bf16[2,2,128,768]{3,2,1,0:T(8,128)(2,1)} %get-tuple-elem, ...), custom_call_target="tpu_custom_call" | custom-call | tf_op jit(solution)/shard_map/results/pallas_call | solution.py:1856

commit v2 on v1

--- a/solution.py
+++ b/solution.py
@@ -973,12 +973,14 @@
         loop(2, one)
 
     def project_ends(seg):
-        both = jnp.concatenate([x[seg, 0:step, :], x[seg, seg_len - step :, :]], axis=0)
+        both = jnp.concatenate(
+            [x[seg, 0:tail, :], jnp.zeros((step - 2 * tail, width), BF), x[seg, seg_len - tail :, :]], axis=0
+        )
 
         def one(j):
             value = nt(wa[j, 0 : 3 * local, :], both)
-            keep_projected(seg, j, slice(0, step), value[:, 0:step])
-            keep_projected(seg, j, slice(seg_len - step, seg_len), value[:, step:])
+            keep_projected(seg, j, slice(0, tail), value[:, 0:tail])
+            keep_projected(seg, j, slice(seg_len - tail, seg_len), value[:, step - tail :])
 
         loop(2, one)
 
@@ -1026,6 +1028,23 @@
         slope = up + active * (1.0 - up) * (2 * c0 + (6 * c0 * 0.044715) * sq)
         r_.gp[seg, :, at] = slope.astype(BF)
 
+    def outer_part(n):
+        def one(i):
+            at = cols(order_at(n))
+            span = half_span(i)[0]
+            part = nn(r_.u[0, span, at], wf[1, at, :])
+            acc[span, :] = jnp.where(n == 0, part, acc[span, :] + part)
+
+        loop(2, one)
+
+    def outer_last():
+        def one(i):
+            at = cols(order[head_count - 1])
+            span = (rows(i), i)
+            give(1, span, acc[span[0], :] + nn(r_.u[0, span[0], at], wf[1, at, :]))
+
+        loop(head_count, one)
+
     def outer(seg):
         def one(i):
             span = (rows(i), i)
@@ -1131,13 +1150,15 @@
             pl.when(n == 3)(start_two)
             ffn_ready(n)
             inner(0, cols(order_at(n)))
+            pl.when(n < head_count - 1)(lambda: outer_part(n))
 
         def wide_units():
             loop(2, lambda n: inner(1, pl.ds(pl.multiple_of(n * 2 * chunk, 2 * chunk), 2 * chunk)))
 
         pl.when(seg == 0)(lambda: loop(head_count, units))
         pl.when(seg == 1)(wide_units)
-        outer(seg)
+        pl.when(seg == 0)(outer_last)
+        pl.when(seg == 1)(lambda: outer(1))
         pl.when(seg == 1)(lambda: rows_pass(2))
         norm_two(seg)
 
@@ -1279,7 +1300,7 @@
 
         return parts
 
-    halves = ("a", "b", "c")
+    halves = tuple("abc")
     for n, name in enumerate(halves):
         sums[name] = attention_sum(n)
     sums["v"] = lambda kind: (
@@ -1315,13 +1336,13 @@
         slot = jnp.where(inside, jnp.where(d == 1, 0, jnp.where(d == 2, 4, 1)), jnp.where(d == 1, 0, d))
         to = from_end(jnp.where(inside, jnp.where(d == 1, 0, 2), 1))
         return push(
-            cut(r_.fsend.at[kind, order_at(d)], kind, 0, 0), r_.f_z.at[kind, slot], r_.fz_s.at[kind, d],
+            cut(r_.fsend.at[kind, order_at(d)], kind, 0, 0), r_.f_z.at[kind, slot], r_.fz_s.at[0],
             r_.fz_r.at[kind, slot], device(core, px, py, to),
         )
 
     def z_in(kind, slot):
         return push(
-            cut(r_.fsend.at[kind, z], kind, 0, 0), r_.f_z.at[kind, slot], r_.fz_s.at[kind, 0], r_.fz_r.at[kind, slot],
+            cut(r_.fsend.at[kind, z], kind, 0, 0), r_.f_z.at[kind, slot], r_.fz_s.at[0], r_.fz_r.at[kind, slot],
             sibling,
         )
 
@@ -1352,14 +1373,13 @@
 
     def last_here(name, k):
         buf, dst, _, _ = last[name]
-        return pltpu.make_async_copy(cut(buf.at[k], k, 0, 0).at[core], dst.at[z], r_.last_sem.at["abcv".index(name)])
+        return pltpu.make_async_copy(cut(buf.at[k], k, 0, 0).at[core], dst.at[z], r_.last_sem.at["abcdefv".index(name)])
 
     last = {
-        "a": (r_.asend.at[0], r_.a_z.at[0], r_.az_s.at[0], r_.az_r.at[0]),
-        "b": (r_.asend.at[1], r_.a_z.at[1], r_.az_s.at[1], r_.az_r.at[1]),
-        "c": (r_.asend.at[2], r_.a_z.at[2], r_.az_s.at[2], r_.az_r.at[2]),
         "v": (r_.vsend, r_.v_z, r_.vz_s, r_.vz_r),
     }
+    for n, name in enumerate(halves):
+        last[name] = (r_.asend.at[n], r_.a_z.at[n], r_.az_s.at[n], r_.az_r.at[n])
 
     def last_each(name, here_do, away_do):
         for k in range(2):
@@ -1399,8 +1419,8 @@
         pl.when(d == 1)(lambda: travel(3, (0,)))
 
     keep_tail()
+    pull_two()
     tail_gather(0, 1)
-    pull_two()
     loop(head_count, lambda n: ffn_grads(head_count - 1 - n))
     dbin_pair = push(r_.dbin, r_.dbin_in, r_.pair_s.at[2], r_.pair_r.at[2], sibling)
 
@@ -1468,15 +1488,18 @@
         def travelling():
             for name in halves:
                 start_sum(name, ((1, 0), (1, 1)))
+            end_ffn(1)
 
         pl.when(n == 0)(travelling)
 
+    loop(2, lambda i: pull_rows(0, half_span(i)))
     loop(2, both_planes)
     start_sum("a", ((0, 1), (0, 0)))
+    z_pass(1)
+    by_half(1, pull_x)
+    text_grad(0)
+    back_send(1, 0)
     tail_gather(1, 1)
-    end_ffn(1)
-    loop(2, lambda i: pull_rows(0, half_span(i)))
-    by_half(1, pull_x)
     pull_memory(0)
     dbin_pair.wait()
 
@@ -1533,24 +1556,19 @@
                 small_cut(k, p, h)
     start_sum("v")
     end_ffn(0)
-    z_pass(1)
-    travel("a")
-    start_sum("b", ((0, 1), (0, 0)))
-    text_grad(0)
-    back_send(1, 0)
-    travel("b")
-    start_sum("c", ((0, 1), (0, 0)))
-    travel("c")
+    for n, name in enumerate(halves):
+        travel(name)
+        if n + 1 < len(halves):
+            start_sum(halves[n + 1], ((0, 1), (0, 0)))
     travel("v")
-    end_plane("a")
-    last_each("a", lambda c: c.start(), lambda c: c.start())
-    tail_gather(1, 2)
-    end_plane("b")
-    last_each("b", lambda c: c.start(), lambda c: c.start())
-    end_plane("v")
-    last_each("v", lambda c: c.start(), lambda c: c.start())
-    end_plane("c")
-    last_each("c", lambda c: c.start(), lambda c: c.start())
+    for n, name in enumerate(halves):
+        if n == len(halves) - 1:
+            end_plane("v")
+            last_each("v", lambda c: c.start(), lambda c: c.start())
+        end_plane(name)
+        last_each(name, lambda c: c.start(), lambda c: c.start())
+        if n == 1:
+            tail_gather(1, 2)
 
     results = (
         (r_.win_v, r_.win_o), (r_.wback_v, r_.wback_o), (r_.dt_v, r_.dt_o), (r_.dqkv_v, r_.dqkv_o),
@@ -1580,9 +1598,7 @@
 
 
     sums_sent()
-    for d in range(1, head_count):
-        for kind in range(2):
-            z_out(kind, d).wait_send()
+    sent_rows(2 * (head_count - 1) * hid, r_.fz_s.at[0])
     for which in range(2):
         for seg in range(2):
             back_sent(which, seg)
@@ -1632,7 +1648,7 @@
     leave(4).start()
     for n in range(len(results)):
         leave(n).wait()
-    for name in "abcv":
+    for name in halves + ("v",):
         last_each(name, None, lambda c: c.wait_send())
 
 
@@ -1830,14 +1846,14 @@
         tp_s=dma(2),
         tp_r=dma(2),
         vsum_r=dma(2, 3),
-        fz_s=dma(2, 4),
+        fz_s=dma(1),
         fz_r=dma(2, 5),
         az_s=dma(3, 2, 2),
         az_r=dma(3, 4),
         leave_sem=dma(10),
         vz_s=dma(2, 2),
         vz_r=dma(4),
-        last_sem=dma(4),
+        last_sem=dma(7),
     )
     scratch.update(staged)
     names = tuple(inputs) + tuple(outputs) + tuple(scratch)

time: 167 us -> 167 us (level)
  no operation moved by 1% of the time
where the time goes in v2:
time: 167 us
  Pallas kernels  166 us (99%)
    pallas_call x1, Pallas kernels, by_chip(): pl.pallas_call(functools.partial(main_kernel, names, dp_count, head_count...  163 us

profile of v2, /device:TPU:0, one launch (start us, length us, event | category | flops | bytes accessed | tf_op | source)
XLA Modules:
  0.0 166.8 jit_solution(9344248177096066502)
XLA Ops:
  0.6 163.2 %layer.1 = (bf16[2,2,128,768]{3,2,1,0:T(8,128)(2,1)}, bf16[2,123,2,768]{3,2,1,0:T(2,128)(2,1)}, f32[10,24]{1,0:T(8,128)}, f32[3,96,192]{2,1,0:T(8,128)}, f32[3,2...) custom-call(bf16[2,123,2,768]{3,2,1,0:T(2,128)(2,1)} %bitcast.14, ...), custom_call_target="tpu_custom_call" | custom-call | tf_op jit(solution)/shard_map/layer/pallas_call | solution.py:1860
  163.8 2.8 %results.1 = (bf16[2,2,128,768]{3,2,1,0:T(8,128)(2,1)}, bf16[2,123,2,768]{3,2,1,0:T(2,128)(2,1)}, f32[10,24]{1,0:T(8,128)}, f32[3,96,192]{2,1,0:T(8,128)}, f32[3...) custom-call(bf16[2,2,128,768]{3,2,1,0:T(8,128)(2,1)} %get-tuple-elem, ...), custom_call_target="tpu_custom_call" | custom-call | tf_op jit(solution)/shard_map/results/pallas_call | solution.py:1872
